TPU v7x, 256 devices: a whole 4x4x8 slice. The times are simulated.
256 devices in a mesh: node: 4 (over x), local: 64 (over z, y, core).
Axes of the slice: x: 4, y: 4, z: 8, core: 2. Of those that a mesh axis runs over, the one named last changes fastest.
Arguments:
- query: bfloat16 [32768, 1024], P(('node', 'local')), may hold values from -40 to 40
- key: bfloat16 [32768, 128], P(('node', 'local')), may hold values from -4 to 4
- value: bfloat16 [32768, 128], P(('node', 'local')), may hold values from -6 to 6
- grad_out: bfloat16 [32768, 1024], P(('node', 'local')), may hold values from -6 to 6
- stretch_order: int32 [4, 128], replicated, may hold values from 0 to 127, each once within a row
- reach: int32 [4], replicated, may hold values from 1024 to 2048, as said below
Outputs:
- grad_query: bfloat16 [32768, 1024], P(('node', 'local'))
- grad_key: bfloat16 [32768, 128], P(('node', 'local'))
- grad_value: bfloat16 [32768, 128], P(('node', 'local'))
Inputs may be any that keep to these rules, and one draw needn't show every extreme that they name: `stretch_order`: each row is a permutation of 0 to 127. Some block has reach exactly 2048.
All inputs are finite; a program needn't handle non-finite values.
Results may differ from a plain program's by a relative error of at most 0.04.
Values may be sent and summed in bfloat16 or wider, within the bound.
No kernel may reach another device: no remote copies, remote signals or barrier semaphores. Data moves between devices by JAX's collectives and lax.ppermute only.
A program may use at most 128 MiB of HBM per device.

v0:
```python
import jax
import jax.numpy as jnp
from jax import lax
from jax.sharding import PartitionSpec as P

HEAD_DIM = 128


def from_behind(value, axis, steps):
    count = lax.axis_size(axis)
    leading, last = (max(0, -steps), min(count, count - steps))
    return lax.ppermute(value, axis, [(source, source + steps) for source in range(leading, last)])


def slot_lookup(order, wanted, stretch_count):
    match = order[None, :] == wanted[:, None]
    return jnp.sum(jnp.where(match, jnp.arange(stretch_count, dtype=jnp.int32)[None, :], 0), axis=1)


def per_device(query, key, value, grad_out, stretch_order, reach):
    rows = query.shape[0]
    local_count = lax.axis_size("local")
    block = rows * local_count
    half = rows // 2
    stretch_count = 2 * local_count
    reach_stretches = stretch_count // 4
    window = (reach_stretches + 1) * half
    heads = query.shape[1] // HEAD_DIM
    scale = 1.0 / HEAD_DIM**0.5
    node_idx = lax.axis_index("node")
    local_idx = lax.axis_index("local")
    order_now = lax.dynamic_index_in_dim(stretch_order, node_idx, 0, keepdims=False)
    order_prev = lax.dynamic_index_in_dim(
        stretch_order, jnp.maximum(node_idx - 1, 0), 0, keepdims=False
    )
    reach_now = lax.dynamic_index_in_dim(reach, node_idx, 0, keepdims=False)
    own_stretches = local_idx * 2 + jnp.arange(2, dtype=jnp.int32)
    own_match = own_stretches[:, None] == jnp.arange(stretch_count, dtype=jnp.int32)[None, :]
    own_seq = node_idx * stretch_count + jnp.sum(
        jnp.where(own_match, order_now[None, :], 0), axis=1
    )
    inner = jnp.arange(half, dtype=jnp.int32)
    q_pos = own_seq[:, None] * half + inner[None, :]
    wanted = (
        own_seq[:, None]
        - reach_stretches
        + jnp.arange(reach_stretches + 1, dtype=jnp.int32)[None, :]
    ).reshape(-1)
    in_current = wanted >= node_idx * stretch_count
    slot_now = slot_lookup(order_now, wanted - node_idx * stretch_count, stretch_count)
    slot_before = slot_lookup(order_prev, wanted - (node_idx - 1) * stretch_count, stretch_count)
    picked = jnp.where(in_current, stretch_count + slot_now, slot_before)
    picked = jnp.where(wanted >= 0, picked, 0)
    key_pos = jnp.where(
        (wanted >= 0)[:, None], wanted[:, None] * half + inner[None, :], -1
    ).reshape(2, window)
    cur_keys, cur_values = (
        lax.all_gather(key, "local", axis=0, tiled=True),
        lax.all_gather(value, "local", axis=0, tiled=True),
    )
    prev_keys, prev_values = from_behind((cur_keys, cur_values), "node", 1)
    keys_all = jnp.concatenate([prev_keys, cur_keys], axis=0).reshape(
        2 * stretch_count, half, HEAD_DIM
    )
    values_all = jnp.concatenate([prev_values, cur_values], axis=0).reshape(
        2 * stretch_count, half, HEAD_DIM
    )
    keys_sel = jnp.take(keys_all, picked, axis=0).reshape(2, window, HEAD_DIM)
    values_sel = jnp.take(values_all, picked, axis=0).reshape(2, window, HEAD_DIM)
    query4 = query.reshape(2, half, heads, HEAD_DIM)
    dout4 = grad_out.reshape(2, half, heads, HEAD_DIM)
    raw = jnp.einsum("cthd,ckd->chtk", query4, keys_sel, preferred_element_type=jnp.float32) * scale
    seen = (
        (key_pos[:, None, :] <= q_pos[:, :, None])
        & (key_pos[:, None, :] >= q_pos[:, :, None] - reach_now)
        & (key_pos[:, None, :] >= 0)
    )
    seen = seen[:, None]
    peak = jnp.max(jnp.where(seen, raw, -1e30), axis=-1)
    expd = jnp.where(seen, jnp.exp(raw - peak[..., None]), 0.0)
    total = jnp.sum(expd, axis=-1)
    prob = expd / total[..., None]
    prob_b = prob.astype(jnp.bfloat16)
    attended = jnp.einsum(
        "chtk,ckd->cthd", prob_b, values_sel, preferred_element_type=jnp.float32
    ).astype(jnp.bfloat16)
    delta = jnp.transpose(
        jnp.sum(dout4.astype(jnp.float32) * attended.astype(jnp.float32), axis=-1), (0, 2, 1)
    )
    dprob = jnp.einsum("cthd,ckd->chtk", dout4, values_sel, preferred_element_type=jnp.float32)
    dscore = (prob * (dprob - delta[..., None])).astype(jnp.bfloat16)
    grad_v = jnp.einsum("chtk,cthd->ckd", prob_b, dout4, preferred_element_type=jnp.float32)
    grad_k = (
        jnp.einsum("chtk,cthd->ckd", dscore, query4, preferred_element_type=jnp.float32) * scale
    )
    grad_q = (
        jnp.einsum("chtk,ckd->cthd", dscore, keys_sel, preferred_element_type=jnp.float32) * scale
    )
    empty = jnp.zeros((2 * stretch_count, half, HEAD_DIM), jnp.float32)
    grad_k = (
        empty.at[picked]
        .add(grad_k.reshape(2 * (reach_stretches + 1), half, HEAD_DIM))
        .reshape(2 * block, HEAD_DIM)
    )
    grad_v = (
        empty.at[picked]
        .add(grad_v.reshape(2 * (reach_stretches + 1), half, HEAD_DIM))
        .reshape(2 * block, HEAD_DIM)
    )
    prev_gk = grad_k[:block]
    prev_gv = grad_v[:block]
    cur_gk = grad_k[block:]
    cur_gv = grad_v[block:]
    back_gk, back_gv = (
        from_behind(prev_gk.astype(jnp.bfloat16), "node", -1).astype(prev_gk.dtype),
        from_behind(prev_gv.astype(jnp.bfloat16), "node", -1).astype(prev_gv.dtype),
    )
    sum_gk, sum_gv = (
        lax.psum_scatter(cur_gk + back_gk, "local", scatter_dimension=0, tiled=True),
        lax.psum_scatter(cur_gv + back_gv, "local", scatter_dimension=0, tiled=True),
    )
    grad_query = grad_q.reshape(rows, heads * HEAD_DIM).astype(jnp.bfloat16)
    return (grad_query, sum_gk.astype(jnp.bfloat16), sum_gv.astype(jnp.bfloat16))


def solution(mesh):
    return jax.shard_map(
        per_device,
        mesh=mesh,
        in_specs=(
            P(("node", "local"), None),
            P(("node", "local"), None),
            P(("node", "local"), None),
            P(("node", "local"), None),
            P(),
            P(),
        ),
        out_specs=(
            P(("node", "local"), None),
            P(("node", "local"), None),
            P(("node", "local"), None),
        ),
        check_vma=False,
    )
```

profile of v0, /device:TPU:6, one launch (start us, length us, event | category | flops | bytes accessed | tf_op | source)
XLA Modules:
  0.0 619.3 jit_solution(10127360752751784209)
XLA Ops:
  7.2 0.7 all-gather.5.cloned.1.call-update
  7.9 0.7 all-gather.3.cloned.1.call-update
  8.7 0.8 dynamic-slice_bitcast_fusion
  9.5 0.2 fusion.31
  9.7 0.1 fusion.35
  9.8 0.1 ge.71
  9.8 0.1 ge.79
  9.9 0.1 ge.74
  10.0 0.1 ge.80
  10.1 0.1 fusion.32
  10.2 0.1 sub.64
  10.3 0.1 sub.60
  10.3 1.2 dynamic_slice.13
  11.6 0.1 broadcast_in_dim.107
  11.7 0.1 broadcast_in_dim.108
  11.8 0.1 add.178
  11.8 0.1 add.179
  11.9 0.1 add.181
  12.0 1.7 copy.27
  13.7 1.0 copy.28
  14.7 0.2 select_reduce_fusion
  14.9 76.1 %all-gather.5.cloned.1.call-done = bf16[8192,128]{1,0:T(8,128)(2,1)} async-done(((bf16[128,128]{1,0:T(8,128)(2,1)}), bf16[8192,128]{1,0:T(8,128)(2,1)}) %all-gather.5.cloned.1.call-update) | async-done | bytes 2097168 | tf_op jit(solution)/shard_map/all_gather | solution.py:59
  91.0 1.3 collective-permute-start.1
  92.3 0.7 iota_add_fusion
  93.1 1.1 and_and_fusion
  94.2 74.6 %all-gather.3.cloned.1.call-done = bf16[8192,128]{1,0:T(8,128)(2,1)} async-done(((bf16[128,128]{1,0:T(8,128)(2,1)}), bf16[8192,128]{1,0:T(8,128)(2,1)}) %all-gather.3.cloned.1.call-update) | async-done | bytes 2097168 | tf_op jit(solution)/shard_map/all_gather | solution.py:58
  168.8 1.3 collective-permute-start
  170.1 5.8 pad_maximum_fusion.1
  175.9 2.9 gather_fusion.1
  178.8 40.0 %collective-permute-done = bf16[8192,128]{1,0:T(8,128)(2,1)} collective-permute-done((bf16[8192,128]{1,0:T(8,128)(2,1)}, bf16[8192,128]{1,0:T(8,128)(2,1)}, u32[]{:S(2)}, u32[]{:S(2)}) %collective-permute-start) | collective-permute-done | bytes 2097184 | tf_op jit(solution)/shard_map/ppermute | solution.py:12
  218.8 11.0 %pad_maximum_fusion = bf16[16384,128]{1,0:T(8,128)(2,1)} fusion(bf16[8192,128]{1,0:T(8,128)(2,1)S(1)} %copy-done.3, bf16[8192,128]{1,0:T(8,128)(2,1)} %collective-permute-done), kind=kLoop, calls=%fused_computation.20 | loop fusion | flops 8388608 | bytes 8388608 | tf_op jit(solution)/shard_map/concatenate | solution.py:62
  229.8 2.9 gather_fusion
  232.7 1.3 broadcast_select_fusion
  234.0 7.3 %fusion.41 = (f32[2,8,64]{2,1,0:T(8,128)S(1)}, f32[2,8,64,2112]{3,2,1,0:T(8,128)}) fusion(pred[2,64,2112]{2,1,0:T(8,128)(4,1)} %and_and_fusion, bf16[2,2112,128,1]{2,1,3,0:T(8,128)(2,1)S(1)} %bitcast.96, bf16[2,64,8,128]{3,2,1,0:T(8,128)(2,1)} %bitcast.110), kind=kOutput, calls=%fused_computation.75 | convolution fusion | flops 1120274432 | bytes 10268672 | tf_op jit(solution)/shard_map/sub | solution.py:80
  241.3 4.9 fusion.11
  246.2 1.4 fusion.16
  247.6 1.0 slice-done.1
  248.6 0.4 slice-done.2
  249.0 1.9 fusion.2
  250.9 1.9 fusion.10
  252.8 0.2 copy-done.1
  253.0 4.3 broadcast_in_dim.113.clone
  257.3 11.5 %scatter_fusion = f32[256,64,128]{2,1,0:T(8,128)} fusion(f32[256,64,128]{2,1,0:T(8,128)} %broadcast_in_dim.113.clone, s32[66]{0:T(128)S(1)} %fusion.37, f32[66,64,128]{2,1,0:T(8,128)S(1)} %bitcast.101), kind=kCustom, calls=%fused_computation.2 | custom fusion | flops 540672 | bytes 6488328 | tf_op jit(solution)/shard_map/scatter-add | solution.py:102
  268.8 2.7 slice.39
  271.5 2.9 collective-permute-start.2
  274.4 2.7 slice.32
  277.1 41.6 %collective-permute-done.2 = bf16[8192,128]{1,0:T(8,128)(2,1)S(1)} collective-permute-done((bf16[8192,128]{1,0:T(8,128)(2,1)S(1)}, bf16[8192,128]{1,0:T(8,128)(2,1)S(1)}, u32[]{:S(2)}, u32[]{:S(2)}) %collective-permute-start.2) | collective-permute-done | bytes 2097184 | tf_op jit(solution)/shard_map/ppermute | solution.py:12
  318.8 2.3 bitcast_add_fusion.1
  321.1 0.0 reduce-scatter.5.cloned.1.call-start
  321.2 4.1 fusion.20
  325.3 4.3 broadcast_in_dim.113.clone.1
  329.6 11.6 %scatter_fusion.1 = f32[256,64,128]{2,1,0:T(8,128)} fusion(f32[256,64,128]{2,1,0:T(8,128)} %broadcast_in_dim.113.clone.1, s32[66]{0:T(128)S(1)} %fusion.37, f32[66,64,128]{2,1,0:T(8,128)S(1)} %bitcast.100), kind=kCustom, calls=%fused_computation.3 | custom fusion | flops 540672 | bytes 6488328 | tf_op jit(solution)/shard_map/scatter-add | solution.py:107
  341.2 2.8 slice.38
  343.9 4.6 collective-permute-start.3
  348.5 2.8 slice.34
  351.3 40.6 %collective-permute-done.3 = bf16[8192,128]{1,0:T(8,128)(2,1)S(1)} collective-permute-done((bf16[8192,128]{1,0:T(8,128)(2,1)S(1)}, bf16[8192,128]{1,0:T(8,128)(2,1)S(1)}, u32[]{:S(2)}, u32[]{:S(2)}) %collective-permute-start.3) | collective-permute-done | bytes 2097184 | tf_op jit(solution)/shard_map/ppermute | solution.py:12
  391.9 2.3 bitcast_add_fusion
  394.2 3.5 fusion.17
  397.7 0.2 copy.20
  397.9 0.8 copy.50
  398.7 65.8 %reduce-scatter.3.cloned.1.call-done = f32[128,128]{1,0:T(8,128)} async-done(((f32[8192,128]{1,0:T(8,128)}), f32[128,128]{1,0:T(8,128)}) %reduce-scatter.3.cloned.1.call-update) | async-done | bytes 65552 | tf_op jit(solution)/shard_map/reduce_scatter | solution.py:119
  464.5 1.5 convert_element_type.59
  466.0 145.3 %reduce-scatter.5.cloned.1.call-done = f32[128,128]{1,0:T(8,128)} async-done(((f32[8192,128]{1,0:T(8,128)}), f32[128,128]{1,0:T(8,128)}) %reduce-scatter.5.cloned.1.call-update) | async-done | bytes 65552 | tf_op jit(solution)/shard_map/reduce_scatter | solution.py:120
  611.3 1.5 convert_element_type.62
  (27 shorter events, 0.2 us)
Async XLA Ops:
  7.2 83.8 %all-gather.5.cloned.1.call-start = ((), (), s32[]{:S(2)}) async-start(), calls=%async_computation.3 | async-start | bytes 2129920 | tf_op jit(solution)/shard_map/all_gather | solution.py:59
  7.9 160.9 %all-gather.3.cloned.1.call-start = ((), (), s32[]{:S(2)}) async-start(), calls=%async_computation.2 | async-start | bytes 2129920 | tf_op jit(solution)/shard_map/all_gather | solution.py:58
  8.6 455.9 %reduce-scatter.3.cloned.1.call-start = ((), (), s32[]{:S(2)}) async-start(), calls=%async_computation.4 | async-start | bytes 4259840 | tf_op jit(solution)/shard_map/reduce_scatter | solution.py:119
  91.0 79.1 %collective-permute-start.1 = (bf16[8192,128]{1,0:T(8,128)(2,1)}, bf16[8192,128]{1,0:T(8,128)(2,1)}, u32[]{:S(2)}, u32[]{:S(2)}) collective-permute-start(bf16[8192,128]{1,0:T(8,128)(2,1)} %all-gather.5.cloned.1.call-done), channel_id=1, source_target_pairs={{0,64},{64,128},{128,192},{1,65},{65,129},{129,193},{2,66},{66,130... | collective-permute-start | bytes 6291464 | tf_op jit(solution)/shard_map/ppermute | solution.py:12
  168.8 50.0 %collective-permute-start = (bf16[8192,128]{1,0:T(8,128)(2,1)}, bf16[8192,128]{1,0:T(8,128)(2,1)}, u32[]{:S(2)}, u32[]{:S(2)}) collective-permute-start(bf16[8192,128]{1,0:T(8,128)(2,1)} %all-gather.3.cloned.1.call-done), channel_id=1, source_target_pairs={{0,64},{64,128},{128,192},{1,65},{65,129},{129,193},{2,66},{66,130... | collective-permute-start | bytes 6291464 | tf_op jit(solution)/shard_map/ppermute | solution.py:12
  170.1 48.7 %copy-start.3 = (bf16[8192,128]{1,0:T(8,128)(2,1)S(1)}, bf16[8192,128]{1,0:T(8,128)(2,1)}, u32[]{:S(2)}) copy-start(bf16[8192,128]{1,0:T(8,128)(2,1)} %all-gather.3.cloned.1.call-done) | copy-start | bytes 6291460
  241.3 6.3 %slice-start = ((s8[8912896]{0:T(1024)(128)(4,1)}), s8[4194304]{0:T(1024)(128)(4,1)S(1)}, s32[]{:S(2)}) async-start(s8[8912896]{0:T(1024)(128)(4,1)} %bitcast.92), calls=%async_computation.6 | async-start | bytes 8388608
  241.3 4.9 copy-start.2
  241.3 7.3 %slice-start.1 = ((s8[8912896]{0:T(1024)(128)(4,1)}), s8[4194304]{0:T(1024)(128)(4,1)S(1)}, s32[]{:S(2)}) async-start(s8[8912896]{0:T(1024)(128)(4,1)} %bitcast.92), calls=%async_computation.7 | async-start | bytes 8388608
  241.3 7.7 %slice-start.2 = ((s8[8912896]{0:T(1024)(128)(4,1)}), s8[524288]{0:T(1024)(128)(4,1)S(1)}, s32[]{:S(2)}) async-start(s8[8912896]{0:T(1024)(128)(4,1)} %bitcast.92), calls=%async_computation.8 | async-start | bytes 1048576
  246.2 4.7 copy-start
  249.0 1.9 copy-start.4
  250.9 2.1 copy-start.1
  271.5 47.3 %collective-permute-start.2 = (bf16[8192,128]{1,0:T(8,128)(2,1)S(1)}, bf16[8192,128]{1,0:T(8,128)(2,1)S(1)}, u32[]{:S(2)}, u32[]{:S(2)}) collective-permute-start(bf16[8192,128]{1,0:T(8,128)(2,1)S(1)} %bitcast.102), channel_id=1, source_target_pairs={{64,0},{128,64},{192,128},{65,1},{129,65},{193,129},{66,2},{130,66... | collective-permute-start | bytes 6291464 | tf_op jit(solution)/shard_map/ppermute | solution.py:12
  321.1 290.1 %reduce-scatter.5.cloned.1.call-start = ((), (), s32[]{:S(2)}) async-start(), calls=%async_computation.5 | async-start | bytes 4259840 | tf_op jit(solution)/shard_map/reduce_scatter | solution.py:120
  343.9 47.9 %collective-permute-start.3 = (bf16[8192,128]{1,0:T(8,128)(2,1)S(1)}, bf16[8192,128]{1,0:T(8,128)(2,1)S(1)}, u32[]{:S(2)}, u32[]{:S(2)}) collective-permute-start(bf16[8192,128]{1,0:T(8,128)(2,1)S(1)} %bitcast.103), channel_id=1, source_target_pairs={{64,0},{128,64},{192,128},{65,1},{129,65},{193,129},{66,2},{130,66... | collective-permute-start | bytes 6291464 | tf_op jit(solution)/shard_map/ppermute | solution.py:12
Sparse Core Ops, SparseCore 0:
  10.8 80.1 all-gather.4
  93.8 74.9 all-gather.2
  321.2 143.2 reduce-scatter.2
  469.1 142.1 reduce-scatter.4
where the time goes:
time: 621 us; the launch traced here: 619 us
  waiting for transfers between devices  485 us (78%)
  other arithmetic  56 us (9%)
  local copies, waits for them, and re-layouts  33.5 us (5%)
  matrix products  20.1 us (3%)
  between operations  14.1 us (2%)
  starting transfers between devices  10.2 us (2%)
    reduce_scatter x1, waiting for transfers between devices, per_device(): lax.psum_scatter(cur_gv + back_gv, 'local', scatter_dimension=0, tiled=True)  145 us
    ppermute x4, waiting for transfers between devices, from_behind(): lax.ppermute(value, axis, [(source, source + steps) for source in range(l...  122 us
    all_gather x1, waiting for transfers between devices, per_device(): lax.all_gather(value, 'local', axis=0, tiled=True)  76.1 us
    all_gather x1, waiting for transfers between devices, per_device(): lax.all_gather(key, 'local', axis=0, tiled=True)  74.6 us
    reduce_scatter x1, waiting for transfers between devices, per_device(): lax.psum_scatter(cur_gk + back_gk, 'local', scatter_dimension=0, tiled=True)  65.8 us
  transfers between devices with their start and end apart: 8, of which 7 were waited for; matrix products, arithmetic and copies ran while one was open for 9% of the time, Pallas kernels for 0%

commit v1 on v0

v1 whole, which is shorter than its diff:
```python
import functools

import jax
import jax.numpy as jnp
import numpy as np
from jax import lax
from jax.experimental import pallas as pl
from jax.experimental.pallas import tpu as pltpu
from jax.sharding import PartitionSpec as P

HEAD_DIM = 128
PAIR = 2 * HEAD_DIM
HEADS = 8
STRETCH = 64
SLOTS = 128
BACK = 32
KEYS = BACK + 1
WINDOW = KEYS * STRETCH
COLS = HEADS * STRETCH
CHUNK = 11 * STRETCH
CHUNKS = WINDOW // CHUNK
TAIL = BACK // 2
NZ, NY = 8, 4
LOCAL = NZ * NY * 2
FAR = -1e30

MEMBERS = (((2, 1), (6, 1)), ((6, 3), (2, 3)), ((0, 2), (4, 0)))
OPPOSITE = (4, 2)


def local_of(z, y, c):
    return ((z % NZ) * NY + y % NY) * 2 + c


def moves(by_core):
    out = []
    for source in range(LOCAL):
        z, y, c = source // (NY * 2), (source // 2) % NY, source % 2
        if by_core is None:
            out.append((source, local_of(z, y, 1 - c)))
        else:
            dz, dy = by_core[c]
            out.append((source, local_of(z + dz, y + dy, c)))
    return out


def send(value, by_core):
    return lax.ppermute(value, "local", moves(by_core))


def swap(value):
    return send(value, None)


def shift(value, dz, dy):
    return send(value, ((dz, dy), (dz, dy)))


def gather_block(own, unit, send, join):
    swap = functools.partial(send, by_core=None)
    chip = join([own, swap(own)])
    members = [send(chip, by_core=m) for m in MEMBERS]
    opposite = send(own, by_core=(OPPOSITE, OPPOSITE))
    mine = join([own, opposite] + members)
    half = 4 * unit
    up = send(mine[:half], by_core=((0, 1), (0, 1)))
    down = send(mine[:half], by_core=((0, -1), (0, -1)))
    ahead = send(mine, by_core=((1, 0), (1, 0)))
    behind = send(mine, by_core=((-1, 0), (-1, 0)))
    pieces = [mine, up, down, ahead, behind]
    return pieces + [swap(piece) for piece in pieces]


def piece_table():
    labels = np.arange(SLOTS).reshape(LOCAL, 2).T

    def fake_send(value, by_core):
        out = np.empty_like(value)
        for source, target in moves(by_core):
            out[:, target] = value[:, source]
        return out

    pieces = gather_block(labels, 2, fake_send, lambda parts: np.concatenate(parts, 0))
    order = np.concatenate(pieces, 0).T
    table = np.empty((LOCAL, SLOTS), np.int32)
    for device in range(LOCAL):
        table[device, order[device]] = np.arange(SLOTS)
    return table


TABLE = piece_table()
PIECES = (16, 8, 8, 16, 16) * 2
STARTS = tuple(int(s) for s in np.cumsum((0,) + PIECES))


def pick_kernel(places, *refs):
    pieces, out, sem = refs[: len(PIECES)], refs[-2], refs[-1]

    def start(i, carry):
        place = places[i]
        for piece, first, last in zip(pieces, STARTS[:-1], STARTS[1:]):

            @pl.when((place >= first) & (place < last))
            def _():
                row = pl.multiple_of((place - first) * STRETCH, STRETCH)
                to = pl.multiple_of(i * STRETCH, STRETCH)
                pltpu.make_async_copy(
                    piece.at[pl.ds(row, STRETCH)], out.at[pl.ds(to, STRETCH)], sem.at[i]
                ).start()

        return carry

    lax.fori_loop(0, TAIL, start, 0)
    for i in range(TAIL):
        rows = pl.ds(i * STRETCH, STRETCH)
        pltpu.make_async_copy(pieces[0].at[pl.ds(0, STRETCH)], out.at[rows], sem.at[i]).wait()


def pick(places, pieces):
    return pl.pallas_call(
        pick_kernel,
        out_shape=jax.ShapeDtypeStruct((TAIL * STRETCH, PAIR), jnp.bfloat16),
        in_specs=[pl.BlockSpec(memory_space=pltpu.SMEM)]
        + [pl.BlockSpec(memory_space=pl.ANY)] * len(pieces),
        out_specs=pl.BlockSpec(memory_space=pl.ANY),
        scratch_shapes=[pltpu.SemaphoreType.DMA((TAIL,))],
        name="pick_tail",
    )(places, *pieces)


def attend_kernel(places, facts, query, grad_out, *refs):
    count = len(PIECES) + 2
    pieces = refs[:count]
    grad_query, block_out, tail_own_out, tail_other_out = refs[count : count + 4]
    rows_in, window, q_heads, g_heads, score, dprob, terms, rows_out, sem, out_sem = refs[count + 4 :]
    scale = 1.0 / HEAD_DIM**0.5
    copies, first = [], 0
    for i, piece in enumerate(pieces):
        rows = piece.shape[0]
        copies.append(pltpu.make_async_copy(piece, rows_in.at[pl.ds(first, rows)], sem.at[i]))
        copies[-1].start()
        first += rows

    def clear(i, carry):
        rows_out[pl.ds(pl.multiple_of(i * 256, 256), 256)] = jnp.zeros((256, PAIR), jnp.bfloat16)
        return carry

    lax.fori_loop(0, rows_out.shape[0] // 256, clear, 0)
    for c in range(2):
        for h in range(HEADS):
            into, rows = pl.ds(h * STRETCH, STRETCH), pl.ds(c * STRETCH, STRETCH)
            columns = pl.ds(h * HEAD_DIM, HEAD_DIM)
            q_heads[c, into] = query[rows, columns]
            g_heads[c, into] = grad_out[rows, columns]
    for copy in copies:
        copy.wait()
    reach = facts[4]
    token = lax.broadcasted_iota(jnp.int32, (1, COLS), 1) % STRETCH
    latest = BACK * STRETCH + token

    def stretch(c, carry):
        def fetch(k, carry):
            place = pl.multiple_of(places[c * KEYS + k] * STRETCH, STRETCH)
            window[pl.ds(pl.multiple_of(k * STRETCH, STRETCH), STRETCH)] = rows_in[pl.ds(place, STRETCH)]
            return carry

        lax.fori_loop(0, KEYS, fetch, 0)
        q, g = q_heads[c], g_heads[c]
        earliest = jnp.maximum(latest - reach, facts[2 + c] * STRETCH)

        def scores(j, peak):
            rows = pl.ds(pl.multiple_of(j * CHUNK, CHUNK), CHUNK)
            keys = window[rows, :HEAD_DIM]
            raw = lax.dot_general(keys, q, (((1,), (1,)), ((), ())), preferred_element_type=jnp.float32)
            row = lax.broadcasted_iota(jnp.int32, (CHUNK, COLS), 0) + j * CHUNK
            seen = (row >= earliest) & (row <= latest)
            raw = jnp.where(seen, raw * (scale * 1.4426950408889634), FAR)
            score[rows] = raw
            return jnp.maximum(peak, jnp.max(raw, axis=0, keepdims=True))

        peak = lax.fori_loop(0, CHUNKS, scores, jnp.full((1, COLS), FAR, jnp.float32))

        def sums(j, carry):
            total, delta = carry
            rows = pl.ds(pl.multiple_of(j * CHUNK, CHUNK), CHUNK)
            expd = jnp.exp2(score[rows] - peak)
            score[rows] = expd
            values = window[rows, HEAD_DIM:]
            dp = lax.dot_general(values, g, (((1,), (1,)), ((), ())), preferred_element_type=jnp.float32)
            dprob[rows] = dp
            total = total + jnp.sum(expd, axis=0, keepdims=True)
            delta = delta + jnp.sum(expd * dp, axis=0, keepdims=True)
            return total, delta

        zero = jnp.zeros((1, COLS), jnp.float32)
        total, delta = lax.fori_loop(0, CHUNKS, sums, (zero, zero))
        share = 1.0 / total
        delta = delta * share

        def grads(j, dq):
            rows = pl.ds(pl.multiple_of(j * CHUNK, CHUNK), CHUNK)
            prob = score[rows] * share
            dscore = (prob * (dprob[rows] - delta)).astype(jnp.bfloat16)
            terms[c, rows, HEAD_DIM:] = jnp.dot(
                prob.astype(jnp.bfloat16), g, preferred_element_type=jnp.float32
            )
            terms[c, rows, :HEAD_DIM] = jnp.dot(dscore, q, preferred_element_type=jnp.float32) * scale
            keys = window[rows, :HEAD_DIM]
            return dq + lax.dot_general(
                keys, dscore, (((0,), (0,)), ((), ())), preferred_element_type=jnp.float32
            )

        dq = lax.fori_loop(0, CHUNKS, grads, jnp.zeros((HEAD_DIM, COLS), jnp.float32))
        dq = (jnp.transpose(dq) * scale).astype(jnp.bfloat16)
        for h in range(HEADS):
            grad_query[pl.ds(pl.multiple_of(c * STRETCH, STRETCH), STRETCH), pl.ds(h * HEAD_DIM, HEAD_DIM)] = dq[
                h * STRETCH : (h + 1) * STRETCH
            ]
        return carry

    lax.fori_loop(0, 2, stretch, 0)

    def place_first(k, carry):
        @pl.when(k >= facts[2])
        def _():
            place = pl.multiple_of(places[k] * STRETCH, STRETCH)
            rows = pl.ds(pl.multiple_of(k * STRETCH, STRETCH), STRETCH)
            rows_out[pl.ds(place, STRETCH)] = terms[0, rows].astype(jnp.bfloat16)

        return carry

    lax.fori_loop(0, KEYS, place_first, 0)

    def place_second(k, carry):
        @pl.when(k >= facts[3])
        def _():
            place = pl.multiple_of(places[KEYS + k] * STRETCH, STRETCH)
            rows = pl.ds(pl.multiple_of(k * STRETCH, STRETCH), STRETCH)
            twin = k + facts[1] - facts[0]
            both = (twin >= facts[2]) & (twin < KEYS)
            twin = jnp.clip(twin, 0, KEYS - 1)
            first = terms[0, pl.ds(pl.multiple_of(twin * STRETCH, STRETCH), STRETCH)]
            term = terms[1, rows] + jnp.where(both, first, 0.0)
            rows_out[pl.ds(place, STRETCH)] = term.astype(jnp.bfloat16)

        return carry

    lax.fori_loop(0, KEYS, place_second, 0)
    copies, first = [], 0
    for i, out in enumerate((block_out, tail_own_out, tail_other_out)):
        rows = out.shape[0]
        copies.append(pltpu.make_async_copy(rows_out.at[pl.ds(first, rows)], out, out_sem.at[i]))
        copies[-1].start()
        first += rows
    for copy in copies:
        copy.wait()


def attend(places, facts, query, grad_out, pieces):
    rows = (SLOTS + BACK) * STRETCH
    tail = TAIL * STRETCH
    shape = jax.ShapeDtypeStruct
    smem = pl.BlockSpec(memory_space=pltpu.SMEM)
    vmem = pl.BlockSpec(memory_space=pltpu.VMEM)
    anywhere = pl.BlockSpec(memory_space=pl.ANY)
    return pl.pallas_call(
        attend_kernel,
        out_shape=(
            shape(query.shape, jnp.bfloat16),
            shape((SLOTS * STRETCH, PAIR), jnp.bfloat16),
            shape((tail, PAIR), jnp.bfloat16),
            shape((tail, PAIR), jnp.bfloat16),
        ),
        in_specs=[smem, smem, vmem, vmem] + [anywhere] * len(pieces),
        out_specs=(vmem, anywhere, anywhere, anywhere),
        scratch_shapes=[
            pltpu.VMEM((rows, PAIR), jnp.bfloat16),
            pltpu.VMEM((WINDOW, PAIR), jnp.bfloat16),
            pltpu.VMEM((2, COLS, HEAD_DIM), jnp.bfloat16),
            pltpu.VMEM((2, COLS, HEAD_DIM), jnp.bfloat16),
            pltpu.VMEM((WINDOW, COLS), jnp.float32),
            pltpu.VMEM((WINDOW, COLS), jnp.float32),
            pltpu.VMEM((2, WINDOW, PAIR), jnp.float32),
            pltpu.VMEM((rows, PAIR), jnp.bfloat16),
            pltpu.SemaphoreType.DMA((len(pieces),)),
            pltpu.SemaphoreType.DMA((3,)),
        ],
        compiler_params=pltpu.CompilerParams(vmem_limit_bytes=40 * 2**20),
        name="attend",
    )(places, facts, query, grad_out, *pieces)


def merge_kernel(places, block, tail, *refs):
    outs, held, sem, out_sem = refs[: len(PIECES)], refs[-3], refs[-2], refs[-1]
    copy = pltpu.make_async_copy(block, held, sem.at[0])
    copy.start()
    copy.wait()

    def add(i, carry):
        rows = pl.ds(pl.multiple_of(places[i] * STRETCH, STRETCH), STRETCH)
        term = tail[pl.ds(pl.multiple_of(i * STRETCH, STRETCH), STRETCH)]
        held[rows] = (held[rows].astype(jnp.float32) + term.astype(jnp.float32)).astype(jnp.bfloat16)
        return carry

    lax.fori_loop(0, TAIL, add, 0)
    copies = []
    for i, out in enumerate(outs):
        rows = pl.ds(STARTS[i] * STRETCH, PIECES[i] * STRETCH)
        copies.append(pltpu.make_async_copy(held.at[rows], out, out_sem.at[i]))
        copies[-1].start()
    for copy in copies:
        copy.wait()


def merge(places, block, tail):
    anywhere = pl.BlockSpec(memory_space=pl.ANY)
    return pl.pallas_call(
        merge_kernel,
        out_shape=tuple(jax.ShapeDtypeStruct((n * STRETCH, PAIR), jnp.bfloat16) for n in PIECES),
        in_specs=[pl.BlockSpec(memory_space=pltpu.SMEM), anywhere, pl.BlockSpec(memory_space=pltpu.VMEM)],
        out_specs=(anywhere,) * len(PIECES),
        scratch_shapes=[
            pltpu.VMEM(block.shape, jnp.bfloat16),
            pltpu.SemaphoreType.DMA((1,)),
            pltpu.SemaphoreType.DMA((len(PIECES),)),
        ],
        compiler_params=pltpu.CompilerParams(vmem_limit_bytes=16 * 2**20),
        name="merge_tail",
    )(places, block, tail)


def wide(value):
    return value.astype(jnp.float32)


def reduce_block(pieces, unit):
    own, other = pieces[:5], pieces[5:]
    arrived = [swap(piece) for piece in other]
    sums = [wide(a) + wide(b) for a, b in zip(own, arrived)]
    mine, up, down, ahead, behind = [sums[0]] + [s.astype(jnp.bfloat16) for s in sums[1:]]
    ahead, behind = shift(ahead, -1, 0), shift(behind, 1, 0)
    up, down = shift(up, 0, -1), shift(down, 0, 1)
    half = up.shape[0]
    mine = mine + wide(ahead) + wide(behind)
    mine = jnp.concatenate([mine[:half] + wide(up) + wide(down), mine[half:]], 0)
    mine_b = mine.astype(jnp.bfloat16)
    back = []
    for i, by_core in enumerate(MEMBERS):
        rows = mine_b[(2 + 2 * i) * unit : (4 + 2 * i) * unit]
        back.append(send(rows, tuple((-dz, -dy) for dz, dy in by_core)))
    opposite = shift(mine_b[unit : 2 * unit], -OPPOSITE[0], -OPPOSITE[1])
    there = sum(wide(b[unit:]) for b in back)
    here = mine[:unit] + wide(opposite) + sum(wide(b[:unit]) for b in back)
    return here + wide(swap(there.astype(jnp.bfloat16)))


def per_device(query, key, value, grad_out, stretch_order, reach):
    unit = query.shape[0]
    node, local = lax.axis_index("node"), lax.axis_index("local")
    core = local % 2
    order = lax.dynamic_index_in_dim(stretch_order, node, 0, keepdims=False)
    table = lax.dynamic_index_in_dim(jnp.asarray(TABLE), local, 0, keepdims=False)
    own = lax.dynamic_slice_in_dim(order, 2 * local, 2)

    def find(wanted):
        match = order[None, :] == wanted[:, None]
        return jnp.sum(jnp.where(match, table[None, :], 0), axis=1)

    wanted = (own[:, None] - BACK + jnp.arange(KEYS, dtype=jnp.int32)[None, :]).reshape(-1)
    tail = wanted + BACK
    in_tail = SLOTS + jnp.where(tail // TAIL == core, 0, TAIL) + tail % TAIL
    places = jnp.where(wanted >= 0, find(wanted), jnp.where(node > 0, in_tail, 0))
    tail_places = find(SLOTS - BACK + core * TAIL + jnp.arange(TAIL, dtype=jnp.int32))
    first_seen = jnp.where(node > 0, 0, jnp.maximum(BACK - own, 0))
    own_reach = lax.dynamic_slice_in_dim(reach, node, 1)
    facts = jnp.concatenate([own, first_seen, own_reach]).astype(jnp.int32)

    pair = jnp.concatenate([key, value], axis=1)
    pieces = gather_block(pair, unit, send, lambda parts: jnp.concatenate(parts, 0))
    nodes = lax.axis_size("node")
    tail_own = lax.ppermute(pick(tail_places, pieces), "node", [(n, n + 1) for n in range(nodes - 1)])
    tail_other = swap(tail_own)
    grad_query, block, back_own, back_other = attend(
        places, facts, query, grad_out, pieces + [tail_own, tail_other]
    )
    back = (wide(back_own) + wide(swap(back_other))).astype(jnp.bfloat16)
    back = lax.ppermute(back, "node", [(n + 1, n) for n in range(nodes - 1)])
    sums = reduce_block(merge(tail_places, block, back), unit).astype(jnp.bfloat16)
    return grad_query, sums[:, :HEAD_DIM], sums[:, HEAD_DIM:]


def solution(mesh):
    rows = P(("node", "local"), None)
    return jax.shard_map(
        per_device,
        mesh=mesh,
        in_specs=(rows, rows, rows, rows, P(), P()),
        out_specs=(rows, rows, rows),
        check_vma=False,
    )
```

time: 621 us -> 165 us (0.27)
  waiting for transfers between devices: 485 us -> 61.2 us
  other arithmetic: 56 us -> 4.17 us
  starting transfers between devices: 10.2 us -> 48.7 us
  Pallas kernels: 0 us -> 33.8 us
  matrix products: 20.1 us -> 0 us
  local copies, waits for them, and re-layouts: 33.5 us -> 14.3 us
  between operations: 14.1 us -> 0.94 us
    reduce_scatter x2 -> x0, waiting for transfers between devices: 211 us -> none  [the longest x1 145 us: per_device(): lax.psum_scatter(cur_gv + back_gv, 'local', scatter_dimension=0, tiled=True)]
    all_gather x2 -> x0, waiting for transfers between devices: 151 us -> none  [the longest x1 76.1 us: per_device(): lax.all_gather(value, 'local', axis=0, tiled=True)]
    ppermute x4 -> x32, waiting for transfers between devices: 122 us -> 61.2 us  [the longest x30 35.6 us: send(): return lax.ppermute(value, 'local', moves(by_core))]
    ppermute x4 -> x32, starting transfers between devices: 10.1 us -> 48.7 us  [the longest x30 44.6 us: send(): return lax.ppermute(value, 'local', moves(by_core))]
    pallas_call x0 -> x3, Pallas kernels: none -> 33.8 us  [the longest x1 17.8 us: pick(): pl.pallas_call(pick_kernel, out_shape=jax.ShapeDtypeStruct((TAIL * STRETC...]
    scatter-add x2 -> x0, other arithmetic: 23.1 us -> none  [the longest x1 11.6 us: per_device(): grad_v = empty.at[picked].add(grad_v.reshape(2 * (reach_stretches + 1), h...]
    concatenate x2 -> x3, other arithmetic: 16.8 us -> 1.45 us  [the longest x2 0.73 us: per_device(): jnp.concatenate(parts, 0)]
    dot_general x5 -> x0, matrix products: 12.8 us -> none  [the longest x1 4.09 us: per_device(): jnp.einsum('chtk,cthd->ckd', prob_b, dout4, preferred_element_type=jnp.fl...]
  transfers between devices with their start and end apart: 8 -> 32, of which waited for: 7 -> 16; matrix products, arithmetic and copies ran while one was open for 9% -> 3% of each run, Pallas kernels for 0% -> 0%
where the time goes in v1:
time: 165 us; the launch traced here: 163 us
  waiting for transfers between devices  61.2 us (37%)
  starting transfers between devices  48.7 us (30%)
  Pallas kernels  33.8 us (20%)
  local copies, waits for them, and re-layouts  14.3 us (9%)
  other arithmetic  4.17 us (3%)
    ppermute x30, starting transfers between devices, send(): return lax.ppermute(value, 'local', moves(by_core))  44.6 us
    ppermute x30, waiting for transfers between devices, send(): return lax.ppermute(value, 'local', moves(by_core))  35.6 us
    pallas_call x1, Pallas kernels, pick(): pl.pallas_call(pick_kernel, out_shape=jax.ShapeDtypeStruct((TAIL * STRETC...  17.8 us
    pallas_call x1, Pallas kernels, attend(): pl.pallas_call(attend_kernel, out_shape=(shape(query.shape, jnp.bfloat16)...  14.6 us
    ppermute x1, waiting for transfers between devices, per_device(): lax.ppermute(pick(tail_places, pieces), 'node', [(n, n + 1) for n in rang...  14 us
    ppermute x1, waiting for transfers between devices, per_device(): back = lax.ppermute(back, 'node', [(n + 1, n) for n in range(nodes - 1)])  11.6 us
    unnamed x40, local copies, waits for them, and re-layouts  11.5 us
  transfers between devices with their start and end apart: 32, of which 16 were waited for; matrix products, arithmetic and copies ran while one was open for 3% of the time, Pallas kernels for 0%

profile of v1, /device:TPU:6, one launch (start us, length us, event | category | flops | bytes accessed | tf_op | source)
XLA Modules:
  0.0 163.1 jit_solution(1667894794666194100)
XLA Ops:
  0.6 0.8 constant_dynamic-update-slice_fusion.1
  1.4 0.8 constant_dynamic-update-slice_fusion
  2.3 9.9 %collective-permute-start = (bf16[128,256]{1,0:T(8,128)(2,1)S(1)}, bf16[128,256]{1,0:T(8,128)(2,1)S(1)}, u32[]{:S(2)}, u32[]{:S(2)}) collective-permute-start(bf16[128,256]{1,0:T(8,128)(2,1)S(1)} %get-tuple-element.41), channel_id=1, source_target_pairs={{0,36},{1,37},{2,38},{3,39},{4,32},{5,33},{6,34},{7,35},{8,44},{9,... | collective-permute-start | bytes 196616 | tf_op jit(solution)/shard_map/ppermute | solution.py:48
  12.2 1.7 %collective-permute-start.2 = (bf16[256,256]{1,0:T(8,128)(2,1)S(1)}, bf16[256,256]{1,0:T(8,128)(2,1)S(1)}, u32[]{:S(2)}, u32[]{:S(2)}) collective-permute-start(bf16[256,256]{1,0:T(8,128)(2,1)S(1)} %pad_maximum_fusion.1), channel_id=1, source_target_pairs={{0,18},{1,51},{2,20},{3,53},{4,22},{5,55},{6,16},{7,49},{8,26},{9,... | collective-permute-start | bytes 393224 | tf_op jit(solution)/shard_map/ppermute | solution.py:48
  13.9 1.8 %collective-permute-start.4 = (bf16[256,256]{1,0:T(8,128)(2,1)S(1)}, bf16[256,256]{1,0:T(8,128)(2,1)S(1)}, u32[]{:S(2)}, u32[]{:S(2)}) collective-permute-start(bf16[256,256]{1,0:T(8,128)(2,1)S(1)} %pad_maximum_fusion.1), channel_id=1, source_target_pairs={{0,4},{1,33},{2,6},{3,35},{4,0},{5,37},{6,2},{7,39},{8,12},{9,41},... | collective-permute-start | bytes 393224 | tf_op jit(solution)/shard_map/ppermute | solution.py:48
  15.7 2.8 %collective-permute-start.3 = (bf16[256,256]{1,0:T(8,128)(2,1)S(1)}, bf16[256,256]{1,0:T(8,128)(2,1)S(1)}, u32[]{:S(2)}, u32[]{:S(2)}) collective-permute-start(bf16[256,256]{1,0:T(8,128)(2,1)S(1)} %pad_maximum_fusion.1), channel_id=1, source_target_pairs={{0,54},{1,23},{2,48},{3,17},{4,50},{5,19},{6,52},{7,21},{8,62},{9,... | collective-permute-start | bytes 393224 | tf_op jit(solution)/shard_map/ppermute | solution.py:48
  18.6 5.5 %collective-permute-done.2 = bf16[256,256]{1,0:T(8,128)(2,1)S(1)} collective-permute-done((bf16[256,256]{1,0:T(8,128)(2,1)S(1)}, bf16[256,256]{1,0:T(8,128)(2,1)S(1)}, u32[]{:S(2)}, u32[]{:S(2)}) %collective-permute-start.2) | collective-permute-done | bytes 131104 | tf_op jit(solution)/shard_map/ppermute | solution.py:48
  24.0 1.4 collective-permute-done.3
  25.4 3.1 %collective-permute-start.8 = (bf16[1024,256]{1,0:T(8,128)(2,1)S(1)}, bf16[1024,256]{1,0:T(8,128)(2,1)S(1)}, u32[]{:S(2)}, u32[]{:S(2)}) collective-permute-start(bf16[1024,256]{1,0:T(8,128)(2,1)S(1)} %constant_dynamic-update-slice_fusion.2.refs_0_), channel_id=1, source_target_pairs={{0,56},{1,57},{2,58},{3,59},{4,60},{5,61},{6,62},{7,63},{8,0},{9,1... | collective-permute-start | bytes 1572872 | tf_op jit(solution)/shard_map/ppermute | solution.py:48
  28.5 0.7 pad_maximum_fusion
  29.2 2.5 %collective-permute-start.6 = (bf16[512,256]{1,0:T(8,128)(2,1)}, bf16[512,256]{1,0:T(8,128)(2,1)S(1)}, u32[]{:S(2)}, u32[]{:S(2)}) collective-permute-start(bf16[512,256]{1,0:T(8,128)(2,1)} %pad_maximum_fusion), channel_id=1, source_target_pairs={{0,6},{1,7},{2,0},{3,1},{4,2},{5,3},{6,4},{7,5},{8,14},{9,15},{10,... | collective-permute-start | bytes 786440 | tf_op jit(solution)/shard_map/ppermute | solution.py:48
  31.7 7.5 %collective-permute-done.8.refs_4_ = bf16[1024,256]{1,0:T(8,128)(2,1)S(1)} collective-permute-done((bf16[1024,256]{1,0:T(8,128)(2,1)S(1)}, bf16[1024,256]{1,0:T(8,128)(2,1)S(1)}, u32[]{:S(2)}, u32[]{:S(2)}) %collective-permute-start.8) | collective-permute-done | bytes 524320 | tf_op jit(solution)/shard_map/ppermute | solution.py:48
  39.2 1.8 %collective-permute-done.7.refs_3_ = bf16[1024,256]{1,0:T(8,128)(2,1)S(1)} collective-permute-done((bf16[1024,256]{1,0:T(8,128)(2,1)S(1)}, bf16[1024,256]{1,0:T(8,128)(2,1)S(1)}, u32[]{:S(2)}, u32[]{:S(2)}) %collective-permute-start.7) | collective-permute-done | bytes 524320 | tf_op jit(solution)/shard_map/ppermute | solution.py:48
  41.0 0.5 collective-permute-start.11
  41.6 0.7 dynamic-slice_bitcast_fusion
  42.3 0.7 select_reduce_fusion.1.places
  43.0 0.8 collective-permute-done.11.refs_7_
  43.8 0.2 collective-permute-done.10.refs_6_
  44.0 0.7 copy-done.8
  44.8 0.8 copy-done.10
  45.6 17.8 %pick_tail.1 = bf16[1024,256]{1,0:T(8,128)(2,1)} custom-call(s32[16]{0:T(128)} %select_reduce_fusion.1.places, bf16[1024,256]{1,0:T(8,128)(2,1)} %copy-done, bf16[512,256]{1,0:T(8,128)(2,1)} %collective-permute-done.5.refs_1_, bf16[512,256]{1,0:T(8,128)(2,1)} %copy-done.12, bf16[1024,256]{1,0:T(8,128)(2,1)} %copy-done.4, bf16[1024,256]{1,0:T(8,128)(2,1)} %copy-done.2, ...), custom_call_target="tpu_custom_call" | custom-call | tf_op jit(solution)/shard_map/pick_tail/pallas_call | solution.py:120
  63.4 1.3 collective-permute-start.14
  64.7 0.8 broadcast_select_fusion
  65.5 14.0 %collective-permute-done.14.refs_10_ = bf16[1024,256]{1,0:T(8,128)(2,1)S(1)} collective-permute-done((bf16[1024,256]{1,0:T(8,128)(2,1)}, bf16[1024,256]{1,0:T(8,128)(2,1)S(1)}, u32[]{:S(2)}, u32[]{:S(2)}) %collective-permute-start.14) | collective-permute-done | bytes 524320 | tf_op jit(solution)/shard_map/ppermute | solution.py:381
  79.5 0.6 dynamic_slice.17
  80.2 0.7 pad_add_fusion.facts
  80.9 0.2 select_reduce_fusion
  81.1 0.2 collective-permute-done.15.refs_11_
  81.4 1.0 copy-done.1
  82.4 1.0 copy-done.3
  83.5 1.0 copy-done.5
  84.5 1.0 copy-done.7
  85.5 1.0 copy-done.9
  86.6 1.0 copy-done.11
  87.6 0.9 copy-done.13
  88.6 0.9 copy-done.14
  89.5 0.9 copy-done.15
  90.5 14.6 %attend.1 = (bf16[128,1024]{1,0:T(8,128)(2,1)}, bf16[8192,256]{1,0:T(8,128)(2,1)S(1)}, bf16[1024,256]{1,0:T(8,128)(2,1)S(1)}, bf16[1024,256]{1,0:T(8,128)(2,1)S(1)}) custom-call(s32[66]{0:T(128)S(1)} %compare_select_fusion.1.places, s32[5]{0:T(128)S(1)} %pad_add_fusion.facts, bf16[128,1024]{1,0:T(8,128)(2,1)S(1)} %copy-done.14, ...), custom_call_target="tpu_custom_call" | custom-call | tf_op jit(solution)/shard_map/attend/pallas_call | solution.py:266
  105.1 0.4 collective-permute-start.16
  105.4 1.6 %collective-permute-done.16 = bf16[1024,256]{1,0:T(8,128)(2,1)S(1)} collective-permute-done((bf16[1024,256]{1,0:T(8,128)(2,1)S(1)}, bf16[1024,256]{1,0:T(8,128)(2,1)S(1)}, u32[]{:S(2)}, u32[]{:S(2)}) %collective-permute-start.16) | collective-permute-done | bytes 524320 | tf_op jit(solution)/shard_map/ppermute | solution.py:48
  107.1 0.2 add_convert_fusion.2
  107.2 2.8 %collective-permute-start.17 = (bf16[1024,256]{1,0:T(8,128)(2,1)S(1)}, bf16[1024,256]{1,0:T(8,128)(2,1)S(1)}, u32[]{:S(2)}, u32[]{:S(2)}) collective-permute-start(bf16[1024,256]{1,0:T(8,128)(2,1)S(1)} %add_convert_fusion.2), channel_id=1, source_target_pairs={{64,0},{128,64},{192,128},{65,1},{129,65},{193,129},{66,2},{130,66... | collective-permute-start | bytes 1572872 | tf_op jit(solution)/shard_map/ppermute | solution.py:387
  110.0 11.6 %collective-permute-done.17.tail = bf16[1024,256]{1,0:T(8,128)(2,1)S(1)} collective-permute-done((bf16[1024,256]{1,0:T(8,128)(2,1)S(1)}, bf16[1024,256]{1,0:T(8,128)(2,1)S(1)}, u32[]{:S(2)}, u32[]{:S(2)}) %collective-permute-start.17) | collective-permute-done | bytes 524320 | tf_op jit(solution)/shard_map/ppermute | solution.py:387
  121.6 1.4 merge_tail.1
  123.1 0.5 collective-permute-start.21
  123.7 0.4 collective-permute-start.18
  124.1 0.9 collective-permute-done.19
  125.0 0.1 add_convert_fusion.1
  125.2 1.6 collective-permute-start.20
  126.8 0.1 add_convert_fusion
  126.9 0.6 collective-permute-start.22
  127.6 3.5 %collective-permute-start.24 = (bf16[512,256]{1,0:T(8,128)(2,1)S(1)}, bf16[512,256]{1,0:T(8,128)(2,1)S(1)}, u32[]{:S(2)}, u32[]{:S(2)}) collective-permute-start(bf16[512,256]{1,0:T(8,128)(2,1)S(1)} %add_convert_fusion.4), channel_id=1, source_target_pairs={{0,6},{1,7},{2,0},{3,1},{4,2},{5,3},{6,4},{7,5},{8,14},{9,15},{10,... | collective-permute-start | bytes 786440 | tf_op jit(solution)/shard_map/ppermute | solution.py:48
  131.3 7.9 %collective-permute-done.20 = bf16[1024,256]{1,0:T(8,128)(2,1)S(1)} collective-permute-done((bf16[1024,256]{1,0:T(8,128)(2,1)S(1)}, bf16[1024,256]{1,0:T(8,128)(2,1)S(1)}, u32[]{:S(2)}, u32[]{:S(2)}) %collective-permute-start.20) | collective-permute-done | bytes 524320 | tf_op jit(solution)/shard_map/ppermute | solution.py:48
  139.2 2.7 %collective-permute-done.22 = bf16[1024,256]{1,0:T(8,128)(2,1)S(1)} collective-permute-done((bf16[1024,256]{1,0:T(8,128)(2,1)S(1)}, bf16[1024,256]{1,0:T(8,128)(2,1)S(1)}, u32[]{:S(2)}, u32[]{:S(2)}) %collective-permute-start.22) | collective-permute-done | bytes 524320 | tf_op jit(solution)/shard_map/ppermute | solution.py:48
  141.9 0.3 fusion.8
  142.2 0.5 collective-permute-start.29
  142.7 3.0 %collective-permute-start.30 = (bf16[256,256]{1,0:T(8,128)(2,1)S(1)}, bf16[256,256]{1,0:T(8,128)(2,1)S(1)}, u32[]{:S(2)}, u32[]{:S(2)}) collective-permute-start(bf16[256,256]{1,0:T(8,128)(2,1)S(1)} %get-tuple-element.38), channel_id=1, source_target_pairs={{0,4},{1,33},{2,6},{3,35},{4,0},{5,37},{6,2},{7,39},{8,12},{9,41},... | collective-permute-start | bytes 393224 | tf_op jit(solution)/shard_map/ppermute | solution.py:48
  145.8 5.6 %collective-permute-start.28 = (bf16[256,256]{1,0:T(8,128)(2,1)S(1)}, bf16[256,256]{1,0:T(8,128)(2,1)S(1)}, u32[]{:S(2)}, u32[]{:S(2)}) collective-permute-start(bf16[256,256]{1,0:T(8,128)(2,1)S(1)} %slice.70), channel_id=1, source_target_pairs={{0,54},{1,23},{2,48},{3,17},{4,50},{5,19},{6,52},{7,21},{8,62},{9,... | collective-permute-start | bytes 393224 | tf_op jit(solution)/shard_map/ppermute | solution.py:48
  151.4 3.3 %collective-permute-start.27 = (bf16[128,256]{1,0:T(8,128)(2,1)S(1)}, bf16[128,256]{1,0:T(8,128)(2,1)S(1)}, u32[]{:S(2)}, u32[]{:S(2)}) collective-permute-start(bf16[128,256]{1,0:T(8,128)(2,1)S(1)} %slice.69), channel_id=1, source_target_pairs={{0,36},{1,37},{2,38},{3,39},{4,32},{5,33},{6,34},{7,35},{8,44},{9,... | collective-permute-start | bytes 196616 | tf_op jit(solution)/shard_map/ppermute | solution.py:48
  154.7 0.8 collective-permute-done.29
  155.5 2.1 %collective-permute-done.28 = bf16[256,256]{1,0:T(8,128)(2,1)S(1)} collective-permute-done((bf16[256,256]{1,0:T(8,128)(2,1)S(1)}, bf16[256,256]{1,0:T(8,128)(2,1)S(1)}, u32[]{:S(2)}, u32[]{:S(2)}) %collective-permute-start.28) | collective-permute-done | bytes 131104 | tf_op jit(solution)/shard_map/ppermute | solution.py:48
  157.6 2.4 %collective-permute-start.31 = (bf16[128,256]{1,0:T(8,128)(2,1)S(1)}, bf16[128,256]{1,0:T(8,128)(2,1)S(1)}, u32[]{:S(2)}, u32[]{:S(2)}) collective-permute-start(bf16[128,256]{1,0:T(8,128)(2,1)S(1)} %add_convert_fusion.5), channel_id=1, source_target_pairs={{0,1},{1,0},{2,3},{3,2},{4,5},{5,4},{6,7},{7,6},{8,9},{9,8},{10,11... | collective-permute-start | bytes 196616 | tf_op jit(solution)/shard_map/ppermute | solution.py:48
  160.0 2.4 %collective-permute-done.27 = bf16[128,256]{1,0:T(8,128)(2,1)S(1)} collective-permute-done((bf16[128,256]{1,0:T(8,128)(2,1)S(1)}, bf16[128,256]{1,0:T(8,128)(2,1)S(1)}, u32[]{:S(2)}, u32[]{:S(2)}) %collective-permute-start.27) | collective-permute-done | bytes 65568 | tf_op jit(solution)/shard_map/ppermute | solution.py:48
  162.4 0.6 fusion.10
  (71 shorter events, 1.1 us)
Async XLA Ops:
  0.6 78.9 %copy-start.17 = (s32[4]{0:T(128)S(1)}, s32[4]{0:T(128)}, u32[]{:S(2)}) copy-start(s32[4]{0:T(128)} %param.12) | copy-start | bytes 52
  2.2 10.0 %collective-permute-start.1 = (bf16[128,256]{1,0:T(8,128)(2,1)S(1)}, bf16[128,256]{1,0:T(8,128)(2,1)S(1)}, u32[]{:S(2)}, u32[]{:S(2)}) collective-permute-start(bf16[128,256]{1,0:T(8,128)(2,1)S(1)} %get-tuple-element.41), channel_id=1, source_target_pairs={{0,1},{1,0},{2,3},{3,2},{4,5},{5,4},{6,7},{7,6},{8,9},{9,8},{10,11... | collective-permute-start | bytes 196616 | tf_op jit(solution)/shard_map/ppermute | solution.py:48
  2.3 16.3 %collective-permute-start = (bf16[128,256]{1,0:T(8,128)(2,1)S(1)}, bf16[128,256]{1,0:T(8,128)(2,1)S(1)}, u32[]{:S(2)}, u32[]{:S(2)}) collective-permute-start(bf16[128,256]{1,0:T(8,128)(2,1)S(1)} %get-tuple-element.41), channel_id=1, source_target_pairs={{0,36},{1,37},{2,38},{3,39},{4,32},{5,33},{6,34},{7,35},{8,44},{9,... | collective-permute-start | bytes 196616 | tf_op jit(solution)/shard_map/ppermute | solution.py:48
  12.2 11.8 %collective-permute-start.2 = (bf16[256,256]{1,0:T(8,128)(2,1)S(1)}, bf16[256,256]{1,0:T(8,128)(2,1)S(1)}, u32[]{:S(2)}, u32[]{:S(2)}) collective-permute-start(bf16[256,256]{1,0:T(8,128)(2,1)S(1)} %pad_maximum_fusion.1), channel_id=1, source_target_pairs={{0,18},{1,51},{2,20},{3,53},{4,22},{5,55},{6,16},{7,49},{8,26},{9,... | collective-permute-start | bytes 393224 | tf_op jit(solution)/shard_map/ppermute | solution.py:48
  13.9 11.5 %collective-permute-start.4 = (bf16[256,256]{1,0:T(8,128)(2,1)S(1)}, bf16[256,256]{1,0:T(8,128)(2,1)S(1)}, u32[]{:S(2)}, u32[]{:S(2)}) collective-permute-start(bf16[256,256]{1,0:T(8,128)(2,1)S(1)} %pad_maximum_fusion.1), channel_id=1, source_target_pairs={{0,4},{1,33},{2,6},{3,35},{4,0},{5,37},{6,2},{7,39},{8,12},{9,41},... | collective-permute-start | bytes 393224 | tf_op jit(solution)/shard_map/ppermute | solution.py:48
  15.7 9.7 %collective-permute-start.3 = (bf16[256,256]{1,0:T(8,128)(2,1)S(1)}, bf16[256,256]{1,0:T(8,128)(2,1)S(1)}, u32[]{:S(2)}, u32[]{:S(2)}) collective-permute-start(bf16[256,256]{1,0:T(8,128)(2,1)S(1)} %pad_maximum_fusion.1), channel_id=1, source_target_pairs={{0,54},{1,23},{2,48},{3,17},{4,50},{5,19},{6,52},{7,21},{8,62},{9,... | collective-permute-start | bytes 393224 | tf_op jit(solution)/shard_map/ppermute | solution.py:48
  25.4 18.5 %copy-start = (bf16[1024,256]{1,0:T(8,128)(2,1)}, bf16[1024,256]{1,0:T(8,128)(2,1)S(1)}, u32[]{:S(2)}) copy-start(bf16[1024,256]{1,0:T(8,128)(2,1)S(1)} %constant_dynamic-update-slice_fusion.2.refs_0_) | copy-start | bytes 1572868
  25.4 13.8 %collective-permute-start.8 = (bf16[1024,256]{1,0:T(8,128)(2,1)S(1)}, bf16[1024,256]{1,0:T(8,128)(2,1)S(1)}, u32[]{:S(2)}, u32[]{:S(2)}) collective-permute-start(bf16[1024,256]{1,0:T(8,128)(2,1)S(1)} %constant_dynamic-update-slice_fusion.2.refs_0_), channel_id=1, source_target_pairs={{0,56},{1,57},{2,58},{3,59},{4,60},{5,61},{6,62},{7,63},{8,0},{9,1... | collective-permute-start | bytes 1572872 | tf_op jit(solution)/shard_map/ppermute | solution.py:48
  28.5 12.4 %collective-permute-start.7 = (bf16[1024,256]{1,0:T(8,128)(2,1)S(1)}, bf16[1024,256]{1,0:T(8,128)(2,1)S(1)}, u32[]{:S(2)}, u32[]{:S(2)}) collective-permute-start(bf16[1024,256]{1,0:T(8,128)(2,1)S(1)} %constant_dynamic-update-slice_fusion.2.refs_0_), channel_id=1, source_target_pairs={{0,8},{1,9},{2,10},{3,11},{4,12},{5,13},{6,14},{7,15},{8,16},{9,17... | collective-permute-start | bytes 1572872 | tf_op jit(solution)/shard_map/ppermute | solution.py:48
  29.2 11.7 %collective-permute-start.6 = (bf16[512,256]{1,0:T(8,128)(2,1)}, bf16[512,256]{1,0:T(8,128)(2,1)S(1)}, u32[]{:S(2)}, u32[]{:S(2)}) collective-permute-start(bf16[512,256]{1,0:T(8,128)(2,1)} %pad_maximum_fusion), channel_id=1, source_target_pairs={{0,6},{1,7},{2,0},{3,1},{4,2},{5,3},{6,4},{7,5},{8,14},{9,15},{10,... | collective-permute-start | bytes 786440 | tf_op jit(solution)/shard_map/ppermute | solution.py:48
  31.7 9.7 %collective-permute-start.5 = (bf16[512,256]{1,0:T(8,128)(2,1)}, bf16[512,256]{1,0:T(8,128)(2,1)}, u32[]{:S(2)}, u32[]{:S(2)}) collective-permute-start(bf16[512,256]{1,0:T(8,128)(2,1)} %pad_maximum_fusion), channel_id=1, source_target_pairs={{0,2},{1,3},{2,4},{3,5},{4,6},{5,7},{6,0},{7,1},{8,10},{9,11},{10,... | collective-permute-start | bytes 786440 | tf_op jit(solution)/shard_map/ppermute | solution.py:48
  31.7 11.2 %collective-permute-start.9 = (bf16[1024,256]{1,0:T(8,128)(2,1)S(1)}, bf16[1024,256]{1,0:T(8,128)(2,1)S(1)}, u32[]{:S(2)}, u32[]{:S(2)}) collective-permute-start(bf16[1024,256]{1,0:T(8,128)(2,1)S(1)} %constant_dynamic-update-slice_fusion.2.refs_0_), channel_id=1, source_target_pairs={{0,1},{1,0},{2,3},{3,2},{4,5},{5,4},{6,7},{7,6},{8,9},{9,8},{10,11... | collective-permute-start | bytes 1572872 | tf_op jit(solution)/shard_map/ppermute | solution.py:48
  39.2 4.8 %copy-start.2 = (bf16[1024,256]{1,0:T(8,128)(2,1)}, bf16[1024,256]{1,0:T(8,128)(2,1)S(1)}, u32[]{:S(2)}) copy-start(bf16[1024,256]{1,0:T(8,128)(2,1)S(1)} %collective-permute-done.8.refs_4_) | copy-start | bytes 1572868
  39.2 4.8 %collective-permute-start.13 = (bf16[1024,256]{1,0:T(8,128)(2,1)S(1)}, bf16[1024,256]{1,0:T(8,128)(2,1)S(1)}, u32[]{:S(2)}, u32[]{:S(2)}) collective-permute-start(bf16[1024,256]{1,0:T(8,128)(2,1)S(1)} %collective-permute-done.8.refs_4_), channel_id=1, source_target_pairs={{0,1},{1,0},{2,3},{3,2},{4,5},{5,4},{6,7},{7,6},{8,9},{9,8},{10,11... | collective-permute-start | bytes 1572872 | tf_op jit(solution)/shard_map/ppermute | solution.py:48
  41.0 3.0 %copy-start.4 = (bf16[1024,256]{1,0:T(8,128)(2,1)}, bf16[1024,256]{1,0:T(8,128)(2,1)S(1)}, u32[]{:S(2)}) copy-start(bf16[1024,256]{1,0:T(8,128)(2,1)S(1)} %collective-permute-done.7.refs_3_) | copy-start | bytes 1572868
  41.0 3.0 %collective-permute-start.12 = (bf16[1024,256]{1,0:T(8,128)(2,1)S(1)}, bf16[1024,256]{1,0:T(8,128)(2,1)S(1)}, u32[]{:S(2)}, u32[]{:S(2)}) collective-permute-start(bf16[1024,256]{1,0:T(8,128)(2,1)S(1)} %collective-permute-done.7.refs_3_), channel_id=1, source_target_pairs={{0,1},{1,0},{2,3},{3,2},{4,5},{5,4},{6,7},{7,6},{8,9},{9,8},{10,11... | collective-permute-start | bytes 1572872 | tf_op jit(solution)/shard_map/ppermute | solution.py:48
  41.0 3.0 %copy-start.12 = (bf16[512,256]{1,0:T(8,128)(2,1)}, bf16[512,256]{1,0:T(8,128)(2,1)S(1)}, u32[]{:S(2)}) copy-start(bf16[512,256]{1,0:T(8,128)(2,1)S(1)} %collective-permute-done.6.refs_2_) | copy-start | bytes 786436
  41.0 2.8 %collective-permute-start.11 = (bf16[512,256]{1,0:T(8,128)(2,1)S(1)}, bf16[512,256]{1,0:T(8,128)(2,1)}, u32[]{:S(2)}, u32[]{:S(2)}) collective-permute-start(bf16[512,256]{1,0:T(8,128)(2,1)S(1)} %collective-permute-done.6.refs_2_), channel_id=1, source_target_pairs={{0,1},{1,0},{2,3},{3,2},{4,5},{5,4},{6,7},{7,6},{8,9},{9,8},{10,11... | collective-permute-start | bytes 786440 | tf_op jit(solution)/shard_map/ppermute | solution.py:48
  41.5 2.5 %collective-permute-start.10 = (bf16[512,256]{1,0:T(8,128)(2,1)}, bf16[512,256]{1,0:T(8,128)(2,1)}, u32[]{:S(2)}, u32[]{:S(2)}) collective-permute-start(bf16[512,256]{1,0:T(8,128)(2,1)} %collective-permute-done.5.refs_1_), channel_id=1, source_target_pairs={{0,1},{1,0},{2,3},{3,2},{4,5},{5,4},{6,7},{7,6},{8,9},{9,8},{10,11... | collective-permute-start | bytes 786440 | tf_op jit(solution)/shard_map/ppermute | solution.py:48
  43.0 1.0 copy-start.6
  44.0 0.8 copy-start.8
  44.8 0.8 copy-start.10
  63.4 58.2 %copy-start.16 = (s32[16]{0:T(128)S(1)}, s32[16]{0:T(128)}, u32[]{:S(2)}) copy-start(s32[16]{0:T(128)} %select_reduce_fusion.1.places) | copy-start | bytes 196
  63.4 16.1 %collective-permute-start.14 = (bf16[1024,256]{1,0:T(8,128)(2,1)}, bf16[1024,256]{1,0:T(8,128)(2,1)S(1)}, u32[]{:S(2)}, u32[]{:S(2)}) collective-permute-start(bf16[1024,256]{1,0:T(8,128)(2,1)} %pick_tail.1), channel_id=1, source_target_pairs={{0,64},{64,128},{128,192},{1,65},{65,129},{129,193},{2,66},{66,130... | collective-permute-start | bytes 1572872 | tf_op jit(solution)/shard_map/ppermute | solution.py:381
  79.5 1.9 %collective-permute-start.15 = (bf16[1024,256]{1,0:T(8,128)(2,1)S(1)}, bf16[1024,256]{1,0:T(8,128)(2,1)S(1)}, u32[]{:S(2)}, u32[]{:S(2)}) collective-permute-start(bf16[1024,256]{1,0:T(8,128)(2,1)S(1)} %collective-permute-done.14.refs_10_), channel_id=1, source_target_pairs={{0,1},{1,0},{2,3},{3,2},{4,5},{5,4},{6,7},{7,6},{8,9},{9,8},{10,11... | collective-permute-start | bytes 1572872 | tf_op jit(solution)/shard_map/ppermute | solution.py:48
  81.4 1.0 copy-start.1
  82.4 1.0 copy-start.3
  83.5 1.0 copy-start.5
  84.5 1.0 copy-start.7
  85.5 1.0 copy-start.9
  86.6 1.0 copy-start.11
  87.6 0.9 copy-start.13
  88.6 0.9 copy-start.14
  89.5 0.9 copy-start.15
  105.1 2.0 %collective-permute-start.16 = (bf16[1024,256]{1,0:T(8,128)(2,1)S(1)}, bf16[1024,256]{1,0:T(8,128)(2,1)S(1)}, u32[]{:S(2)}, u32[]{:S(2)}) collective-permute-start(bf16[1024,256]{1,0:T(8,128)(2,1)S(1)} %get-tuple-element.20), channel_id=1, source_target_pairs={{0,1},{1,0},{2,3},{3,2},{4,5},{5,4},{6,7},{7,6},{8,9},{9,8},{10,11... | collective-permute-start | bytes 1572872 | tf_op jit(solution)/shard_map/ppermute | solution.py:48
  107.2 14.3 %collective-permute-start.17 = (bf16[1024,256]{1,0:T(8,128)(2,1)S(1)}, bf16[1024,256]{1,0:T(8,128)(2,1)S(1)}, u32[]{:S(2)}, u32[]{:S(2)}) collective-permute-start(bf16[1024,256]{1,0:T(8,128)(2,1)S(1)} %add_convert_fusion.2), channel_id=1, source_target_pairs={{64,0},{128,64},{192,128},{65,1},{129,65},{193,129},{66,2},{130,66... | collective-permute-start | bytes 1572872 | tf_op jit(solution)/shard_map/ppermute | solution.py:387
  123.0 2.0 %collective-permute-start.19 = (bf16[1024,256]{1,0:T(8,128)(2,1)S(1)}, bf16[1024,256]{1,0:T(8,128)(2,1)S(1)}, u32[]{:S(2)}, u32[]{:S(2)}) collective-permute-start(bf16[1024,256]{1,0:T(8,128)(2,1)S(1)} %get-tuple-element.24), channel_id=1, source_target_pairs={{0,1},{1,0},{2,3},{3,2},{4,5},{5,4},{6,7},{7,6},{8,9},{9,8},{10,11... | collective-permute-start | bytes 1572872 | tf_op jit(solution)/shard_map/ppermute | solution.py:48
  123.1 3.7 %collective-permute-start.21 = (bf16[1024,256]{1,0:T(8,128)(2,1)S(1)}, bf16[1024,256]{1,0:T(8,128)(2,1)S(1)}, u32[]{:S(2)}, u32[]{:S(2)}) collective-permute-start(bf16[1024,256]{1,0:T(8,128)(2,1)S(1)} %get-tuple-element.26), channel_id=1, source_target_pairs={{0,1},{1,0},{2,3},{3,2},{4,5},{5,4},{6,7},{7,6},{8,9},{9,8},{10,11... | collective-permute-start | bytes 1572872 | tf_op jit(solution)/shard_map/ppermute | solution.py:48
  123.6 3.9 %collective-permute-start.23 = (bf16[512,256]{1,0:T(8,128)(2,1)S(1)}, bf16[512,256]{1,0:T(8,128)(2,1)S(1)}, u32[]{:S(2)}, u32[]{:S(2)}) collective-permute-start(bf16[512,256]{1,0:T(8,128)(2,1)S(1)} %get-tuple-element.28), channel_id=1, source_target_pairs={{0,1},{1,0},{2,3},{3,2},{4,5},{5,4},{6,7},{7,6},{8,9},{9,8},{10,11... | collective-permute-start | bytes 786440 | tf_op jit(solution)/shard_map/ppermute | solution.py:48
  123.7 7.6 %collective-permute-start.18 = (bf16[1024,256]{1,0:T(8,128)(2,1)S(1)}, bf16[1024,256]{1,0:T(8,128)(2,1)S(1)}, u32[]{:S(2)}, u32[]{:S(2)}) collective-permute-start(bf16[1024,256]{1,0:T(8,128)(2,1)S(1)} %get-tuple-element.22), channel_id=1, source_target_pairs={{0,1},{1,0},{2,3},{3,2},{4,5},{5,4},{6,7},{7,6},{8,9},{9,8},{10,11... | collective-permute-start | bytes 1572872 | tf_op jit(solution)/shard_map/ppermute | solution.py:48
  125.2 14.0 %collective-permute-start.20 = (bf16[1024,256]{1,0:T(8,128)(2,1)S(1)}, bf16[1024,256]{1,0:T(8,128)(2,1)S(1)}, u32[]{:S(2)}, u32[]{:S(2)}) collective-permute-start(bf16[1024,256]{1,0:T(8,128)(2,1)S(1)} %add_convert_fusion.1), channel_id=1, source_target_pairs={{0,56},{1,57},{2,58},{3,59},{4,60},{5,61},{6,62},{7,63},{8,0},{9,1... | collective-permute-start | bytes 1572872 | tf_op jit(solution)/shard_map/ppermute | solution.py:48
  126.9 15.0 %collective-permute-start.22 = (bf16[1024,256]{1,0:T(8,128)(2,1)S(1)}, bf16[1024,256]{1,0:T(8,128)(2,1)S(1)}, u32[]{:S(2)}, u32[]{:S(2)}) collective-permute-start(bf16[1024,256]{1,0:T(8,128)(2,1)S(1)} %add_convert_fusion), channel_id=1, source_target_pairs={{0,8},{1,9},{2,10},{3,11},{4,12},{5,13},{6,14},{7,15},{8,16},{9,17... | collective-permute-start | bytes 1572872 | tf_op jit(solution)/shard_map/ppermute | solution.py:48
  127.5 3.6 %collective-permute-start.25 = (bf16[512,256]{1,0:T(8,128)(2,1)S(1)}, bf16[512,256]{1,0:T(8,128)(2,1)S(1)}, u32[]{:S(2)}, u32[]{:S(2)}) collective-permute-start(bf16[512,256]{1,0:T(8,128)(2,1)S(1)} %get-tuple-element.30), channel_id=1, source_target_pairs={{0,1},{1,0},{2,3},{3,2},{4,5},{5,4},{6,7},{7,6},{8,9},{9,8},{10,11... | collective-permute-start | bytes 786440 | tf_op jit(solution)/shard_map/ppermute | solution.py:48
  127.6 18.1 %collective-permute-start.24 = (bf16[512,256]{1,0:T(8,128)(2,1)S(1)}, bf16[512,256]{1,0:T(8,128)(2,1)S(1)}, u32[]{:S(2)}, u32[]{:S(2)}) collective-permute-start(bf16[512,256]{1,0:T(8,128)(2,1)S(1)} %add_convert_fusion.4), channel_id=1, source_target_pairs={{0,6},{1,7},{2,0},{3,1},{4,2},{5,3},{6,4},{7,5},{8,14},{9,15},{10,... | collective-permute-start | bytes 786440 | tf_op jit(solution)/shard_map/ppermute | solution.py:48
  131.2 14.5 %collective-permute-start.26 = (bf16[512,256]{1,0:T(8,128)(2,1)S(1)}, bf16[512,256]{1,0:T(8,128)(2,1)S(1)}, u32[]{:S(2)}, u32[]{:S(2)}) collective-permute-start(bf16[512,256]{1,0:T(8,128)(2,1)S(1)} %add_convert_fusion.3), channel_id=1, source_target_pairs={{0,2},{1,3},{2,4},{3,5},{4,6},{5,7},{6,0},{7,1},{8,10},{9,11},{10,... | collective-permute-start | bytes 786440 | tf_op jit(solution)/shard_map/ppermute | solution.py:48
  142.2 13.4 %collective-permute-start.29 = (bf16[256,256]{1,0:T(8,128)(2,1)S(1)}, bf16[256,256]{1,0:T(8,128)(2,1)S(1)}, u32[]{:S(2)}, u32[]{:S(2)}) collective-permute-start(bf16[256,256]{1,0:T(8,128)(2,1)S(1)} %get-tuple-element.37), channel_id=1, source_target_pairs={{0,18},{1,51},{2,20},{3,53},{4,22},{5,55},{6,16},{7,49},{8,26},{9,... | collective-permute-start | bytes 393224 | tf_op jit(solution)/shard_map/ppermute | solution.py:48
  142.7 12.8 %collective-permute-start.30 = (bf16[256,256]{1,0:T(8,128)(2,1)S(1)}, bf16[256,256]{1,0:T(8,128)(2,1)S(1)}, u32[]{:S(2)}, u32[]{:S(2)}) collective-permute-start(bf16[256,256]{1,0:T(8,128)(2,1)S(1)} %get-tuple-element.38), channel_id=1, source_target_pairs={{0,4},{1,33},{2,6},{3,35},{4,0},{5,37},{6,2},{7,39},{8,12},{9,41},... | collective-permute-start | bytes 393224 | tf_op jit(solution)/shard_map/ppermute | solution.py:48
  145.8 11.8 %collective-permute-start.28 = (bf16[256,256]{1,0:T(8,128)(2,1)S(1)}, bf16[256,256]{1,0:T(8,128)(2,1)S(1)}, u32[]{:S(2)}, u32[]{:S(2)}) collective-permute-start(bf16[256,256]{1,0:T(8,128)(2,1)S(1)} %slice.70), channel_id=1, source_target_pairs={{0,54},{1,23},{2,48},{3,17},{4,50},{5,19},{6,52},{7,21},{8,62},{9,... | collective-permute-start | bytes 393224 | tf_op jit(solution)/shard_map/ppermute | solution.py:48
  151.4 11.0 %collective-permute-start.27 = (bf16[128,256]{1,0:T(8,128)(2,1)S(1)}, bf16[128,256]{1,0:T(8,128)(2,1)S(1)}, u32[]{:S(2)}, u32[]{:S(2)}) collective-permute-start(bf16[128,256]{1,0:T(8,128)(2,1)S(1)} %slice.69), channel_id=1, source_target_pairs={{0,36},{1,37},{2,38},{3,39},{4,32},{5,33},{6,34},{7,35},{8,44},{9,... | collective-permute-start | bytes 196616 | tf_op jit(solution)/shard_map/ppermute | solution.py:48
  157.6 4.8 %collective-permute-start.31 = (bf16[128,256]{1,0:T(8,128)(2,1)S(1)}, bf16[128,256]{1,0:T(8,128)(2,1)S(1)}, u32[]{:S(2)}, u32[]{:S(2)}) collective-permute-start(bf16[128,256]{1,0:T(8,128)(2,1)S(1)} %add_convert_fusion.5), channel_id=1, source_target_pairs={{0,1},{1,0},{2,3},{3,2},{4,5},{5,4},{6,7},{7,6},{8,9},{9,8},{10,11... | collective-permute-start | bytes 196616 | tf_op jit(solution)/shard_map/ppermute | solution.py:48

commit v2 on v1

v2 whole, which is shorter than its diff:
```python
import functools

import jax
import jax.numpy as jnp
import numpy as np
from jax import lax
from jax.experimental import pallas as pl
from jax.experimental.pallas import tpu as pltpu
from jax.sharding import PartitionSpec as P

HEAD_DIM = 128
HEADS = 8
STRETCH = 64
SLOTS = 128
BACK = 32
KEYS = BACK + 1
WINDOW = KEYS * STRETCH
COLS = HEADS * STRETCH
CHUNK = 11 * STRETCH
CHUNKS = WINDOW // CHUNK
TAIL = BACK // 2
NZ, NY = 8, 4
LOCAL = NZ * NY * 2
FAR = -1e30

MEMBERS = (((2, 1), (6, 1)), ((6, 3), (2, 3)), ((0, 2), (4, 0)))
OPPOSITE = (4, 2)


def local_of(z, y, c):
    return ((z % NZ) * NY + y % NY) * 2 + c


def moves(by_core):
    out = []
    for source in range(LOCAL):
        z, y, c = source // (NY * 2), (source // 2) % NY, source % 2
        if by_core is None:
            out.append((source, local_of(z, y, 1 - c)))
        else:
            dz, dy = by_core[c]
            out.append((source, local_of(z + dz, y + dy, c)))
    return out


def send(value, by_core):
    return lax.ppermute(value, "local", moves(by_core))


def swap(value):
    return send(value, None)


def shift(value, dz, dy):
    return send(value, ((dz, dy), (dz, dy)))


def gather_block(own, unit, send, join, settle=lambda early, late: late):
    swap = functools.partial(send, by_core=None)
    chip = join([own, swap(own)])
    members = [send(chip, by_core=m) for m in MEMBERS]
    opposite = send(own, by_core=(OPPOSITE, OPPOSITE))
    mine = join([own, settle(members[0], opposite)] + members)
    half = 4 * unit
    up = send(mine[:half], by_core=((0, 1), (0, 1)))
    down = send(mine[:half], by_core=((0, -1), (0, -1)))
    ahead = send(mine, by_core=((1, 0), (1, 0)))
    behind = send(mine, by_core=((-1, 0), (-1, 0)))
    pieces = [mine, up, down, ahead, behind]
    return pieces + [swap(piece) for piece in pieces]


def piece_table():
    labels = np.arange(SLOTS).reshape(LOCAL, 2).T

    def fake_send(value, by_core):
        out = np.empty_like(value)
        for source, target in moves(by_core):
            out[:, target] = value[:, source]
        return out

    pieces = gather_block(labels, 2, fake_send, lambda parts: np.concatenate(parts, 0))
    order = np.concatenate(pieces, 0).T
    table = np.empty((LOCAL, SLOTS), np.int32)
    for device in range(LOCAL):
        table[device, order[device]] = np.arange(SLOTS)
    return table


TABLE = piece_table()
PIECES = (16, 8, 8, 16, 16) * 2
ALL = PIECES + (TAIL, TAIL)
STARTS = tuple(int(s) for s in np.cumsum((0,) + ALL))
KEY_COST = 0
VALUE_COST = 6
VMEM_LIMIT = 36 * 2**20
PICK_KIB = 12 * 1024
MERGE_KIB = 16 * 1024

SMEM = pl.BlockSpec(memory_space=pltpu.SMEM)
VMEM = pl.BlockSpec(memory_space=pltpu.VMEM)


def at(i, size=STRETCH):
    return pl.ds(pl.multiple_of(i * size, size), size)


def shape(rows, columns=HEAD_DIM, dtype=jnp.bfloat16):
    return jax.ShapeDtypeStruct((rows, columns), dtype)


def lay(refs, held, columns=slice(None)):
    first = 0
    for ref in refs:
        held[pl.ds(first, ref.shape[0])] = ref[:, columns]
        first += ref.shape[0]


def small(kib):
    return pltpu.CompilerParams(vmem_limit_bytes=kib * 1024)


def plan_kernel(order, reach, table, places, tail_places, facts, inverse):
    node, local = lax.axis_index("node"), lax.axis_index("local")
    core = local % 2

    def turn(s, carry):
        inverse[order[node, s]] = table[local, s]
        return carry

    lax.fori_loop(0, SLOTS, turn, 0, unroll=8)
    for i in range(TAIL):
        tail_places[i] = inverse[SLOTS - BACK + core * TAIL + i]
    facts[4] = reach[node]
    for c in range(2):
        own = order[node, 2 * local + c]
        facts[c] = own
        first = jnp.where(node > 0, 0, jnp.maximum(BACK - own, 0))
        facts[2 + c] = first

        def find(k, carry, c=c, own=own):
            wanted = own - BACK + k
            tail = jnp.maximum(wanted + BACK, 0)
            half = tail // TAIL
            in_tail = SLOTS + jnp.where(half == core, 0, TAIL) + tail % TAIL
            now = inverse[jnp.maximum(wanted, 0)]
            places[c * KEYS + k] = jnp.where(wanted >= 0, now, jnp.where(node > 0, in_tail, 0))
            return carry

        lax.fori_loop(0, KEYS, find, 0, unroll=3)


def plan(stretch_order, reach):
    return pl.pallas_call(
        plan_kernel,
        out_shape=tuple(jax.ShapeDtypeStruct((n,), jnp.int32) for n in (2 * KEYS, TAIL, 5)),
        in_specs=[SMEM] * 3,
        out_specs=(SMEM,) * 3,
        scratch_shapes=[pltpu.SMEM((SLOTS,), jnp.int32)],
        compiler_params=small(256),
        name="plan",
    )(stretch_order, reach, jnp.asarray(TABLE))


def pick_kernel(places, *refs):
    pieces, keys, values, held = refs[: len(PIECES)], *refs[len(PIECES) :]
    lay(pieces, held)

    def one(i, carry):
        rows = held[at(places[i])]
        keys[at(i)], values[at(i)] = rows[:, :HEAD_DIM], rows[:, HEAD_DIM:]
        return carry

    lax.fori_loop(0, TAIL, one, 0)


def pick(places, pieces):
    return pl.pallas_call(
        pick_kernel,
        out_shape=(shape(TAIL * STRETCH),) * 2,
        in_specs=[SMEM] + [VMEM] * len(pieces),
        out_specs=(VMEM,) * 2,
        scratch_shapes=[pltpu.VMEM((SLOTS * STRETCH, 2 * HEAD_DIM), jnp.bfloat16)],
        compiler_params=small(PICK_KIB),
        name="pick_tail",
    )(places, *pieces)


def stack_heads(array, heads):
    for c in range(2):
        for h in range(HEADS):
            heads[c, pl.ds(h * STRETCH, STRETCH)] = array[
                pl.ds(c * STRETCH, STRETCH), pl.ds(h * HEAD_DIM, HEAD_DIM)
            ]


def fetch(places, c, held, window):
    def one(k, carry):
        window[at(k)] = held[at(places[c * KEYS + k])]
        return carry

    lax.fori_loop(0, KEYS, one, 0, unroll=11)


def spread(places, facts, terms, held):
    def clear(i, carry):
        held[at(i, 256)] = jnp.zeros((256, HEAD_DIM), jnp.bfloat16)
        return carry

    lax.fori_loop(0, held.shape[0] // 256, clear, 0, unroll=8)

    dump = SLOTS + BACK

    def first(k, carry):
        place = jnp.where(k >= facts[2], places[k], dump)
        held[at(place)] = terms[0, at(k)].astype(jnp.bfloat16)
        return carry

    lax.fori_loop(0, KEYS, first, 0, unroll=11)

    def second(k, carry):
        place = jnp.where(k >= facts[3], places[KEYS + k], dump)
        twin = k + facts[1] - facts[0]
        both = (twin >= facts[2]) & (twin < KEYS)
        twin = jnp.clip(twin, 0, KEYS - 1)
        term = terms[1, at(k)] + jnp.where(both, terms[0, at(twin)], 0.0)
        held[at(place)] = term.astype(jnp.bfloat16)
        return carry

    lax.fori_loop(0, KEYS, second, 0, unroll=11)


def give(held, outs):
    first = 0
    for out in outs:
        out[...] = held[pl.ds(first, out.shape[0])]
        first += out.shape[0]


def dot(a, b, over):
    return lax.dot_general(a, b, ((over[:1], over[1:]), ((), ())), preferred_element_type=jnp.float32)


def key_kernel(places, facts, query, grad_out, *refs):
    pieces, refs = refs[: len(ALL)], refs[len(ALL) :]
    prob_out, keys_out, q_heads, g_heads, *outs = refs[:7]
    held, score, terms = refs[7:]
    lay(pieces, held, pl.ds(0, HEAD_DIM))
    scale = 1.4426950408889634 / HEAD_DIM**0.5
    stack_heads(query, q_heads)
    stack_heads(grad_out, g_heads)
    token = lax.broadcasted_iota(jnp.int32, (1, COLS), 1) % STRETCH
    latest = BACK * STRETCH + token

    for c in range(2):
        window = keys_out.at[c]
        fetch(places, c, held, window)
        q, g = q_heads[c], g_heads[c]
        earliest = jnp.maximum(latest - facts[4], facts[2 + c] * STRETCH)
        peaks, totals = [], []
        for j in range(CHUNKS):
            rows = pl.ds(j * CHUNK, CHUNK)
            raw = dot(window[rows], q, (1, 1))
            row = lax.broadcasted_iota(jnp.int32, (CHUNK, COLS), 0) + j * CHUNK
            seen = row >= earliest
            if (j + 1) * CHUNK > BACK * STRETCH:
                seen = seen & (row <= latest)
            raw = jnp.where(seen, raw * scale, FAR)
            score[c, rows] = raw
            peaks.append(jnp.max(raw, axis=0, keepdims=True))
            expd = jnp.exp2(score[c, rows] - peaks[j])
            score[c, rows] = expd
            totals.append(jnp.sum(expd, axis=0, keepdims=True))
        peak = functools.reduce(jnp.maximum, peaks)
        weights = [jnp.exp2(p - peak) for p in peaks]
        share = 1.0 / sum(w * t for w, t in zip(weights, totals))
        for j in range(CHUNKS):
            rows = pl.ds(j * CHUNK, CHUNK)
            prob = (score[c, rows] * (share * weights[j])).astype(jnp.bfloat16)
            prob_out[c, rows] = prob
            terms[c, rows] = dot(prob, g, (1, 0))
    spread(places, facts, terms, held)
    give(held, outs)


def value_kernel(places, facts, prob_in, keys_in, q_heads, g_heads, *refs):
    pieces, refs = refs[: len(ALL)], refs[len(ALL) :]
    grad_query, *outs = refs[:4]
    held, window, dprob, terms = refs[4:]
    lay(pieces[: len(PIECES)], held, pl.ds(HEAD_DIM, HEAD_DIM))
    lay(pieces[len(PIECES) :], held.at[pl.ds(SLOTS * STRETCH, 2 * TAIL * STRETCH)])
    scale = 1.0 / HEAD_DIM**0.5

    for c in range(2):
        fetch(places, c, held, window.at[c])
        q, g = q_heads[c], g_heads[c]
        delta = 0.0
        for j in range(CHUNKS):
            rows = pl.ds(j * CHUNK, CHUNK)
            dp = dot(window[c, rows], g, (1, 1))
            dprob[c, rows] = dp
            delta = delta + jnp.sum(prob_in[c, rows].astype(jnp.float32) * dp, axis=0, keepdims=True)
        dq = 0.0
        for j in range(CHUNKS):
            rows = pl.ds(j * CHUNK, CHUNK)
            prob = prob_in[c, rows].astype(jnp.float32)
            dscore = (prob * (dprob[c, rows] - delta)).astype(jnp.bfloat16)
            terms[c, rows] = dot(dscore, q, (1, 0)) * scale
            dq = dq + dot(keys_in[c, rows], dscore, (0, 0))
        dq = (jnp.transpose(dq) * scale).astype(jnp.bfloat16)
        for h in range(HEADS):
            grad_query[pl.ds(c * STRETCH, STRETCH), pl.ds(h * HEAD_DIM, HEAD_DIM)] = dq[
                h * STRETCH : (h + 1) * STRETCH
            ]
    spread(places, facts, terms, held)
    give(held, outs)


PIECE_SHAPES = tuple(shape(n * STRETCH, 2 * HEAD_DIM) for n in PIECES)
TERM_SHAPES = (shape(SLOTS * STRETCH), shape(TAIL * STRETCH), shape(TAIL * STRETCH))
HEAD_SHAPE = jax.ShapeDtypeStruct((2, COLS, HEAD_DIM), jnp.bfloat16)


def cost(matmuls):
    return pl.CostEstimate(
        flops=matmuls * 4 * WINDOW * COLS * HEAD_DIM, bytes_accessed=matmuls * 2**21, transcendentals=0
    )


def on_keys(places, facts, query, grad_out, pieces):
    return pl.pallas_call(
        key_kernel,
        out_shape=(
            jax.ShapeDtypeStruct((2, WINDOW, COLS), jnp.bfloat16),
            jax.ShapeDtypeStruct((2, WINDOW, HEAD_DIM), jnp.bfloat16),
            HEAD_SHAPE,
            HEAD_SHAPE,
        )
        + TERM_SHAPES,
        in_specs=[SMEM, SMEM] + [VMEM] * (2 + len(pieces)),
        out_specs=(VMEM,) * 7,
        scratch_shapes=[
            pltpu.VMEM(((SLOTS + BACK + 1) * STRETCH, HEAD_DIM), jnp.bfloat16),
            pltpu.VMEM((2, WINDOW, COLS), jnp.float32),
            pltpu.VMEM((2, WINDOW, HEAD_DIM), jnp.float32),
        ],
        compiler_params=pltpu.CompilerParams(vmem_limit_bytes=VMEM_LIMIT),
        cost_estimate=cost(KEY_COST),
        name="on_keys",
    )(places, facts, query, grad_out, *pieces)


def on_values(places, facts, carried, pieces):
    return pl.pallas_call(
        value_kernel,
        out_shape=(shape(2 * STRETCH, HEADS * HEAD_DIM),) + TERM_SHAPES,
        in_specs=[SMEM, SMEM] + [VMEM] * (4 + len(pieces)),
        out_specs=(VMEM,) * 4,
        scratch_shapes=[
            pltpu.VMEM(((SLOTS + BACK + 1) * STRETCH, HEAD_DIM), jnp.bfloat16),
            pltpu.VMEM((2, WINDOW, HEAD_DIM), jnp.bfloat16),
            pltpu.VMEM((2, WINDOW, COLS), jnp.float32),
            pltpu.VMEM((2, WINDOW, HEAD_DIM), jnp.float32),
        ],
        compiler_params=pltpu.CompilerParams(vmem_limit_bytes=VMEM_LIMIT),
        cost_estimate=cost(VALUE_COST),
        name="on_values",
    )(places, facts, *carried, *pieces)


def merge_kernel(places, keys, values, tail_keys, tail_values, *refs):
    outs, held = refs[:-1], refs[-1]
    for i, (block, tail) in enumerate(((keys, tail_keys), (values, tail_values))):
        columns = pl.ds(i * HEAD_DIM, HEAD_DIM)
        held[:, columns] = block[...]

        def one(j, carry, tail=tail, columns=columns):
            rows = at(places[j])
            total = held[rows, columns].astype(jnp.float32) + tail[at(j)].astype(jnp.float32)
            held[rows, columns] = total.astype(jnp.bfloat16)
            return carry

        lax.fori_loop(0, TAIL, one, 0)
    give(held, outs)


def merge(places, *arrays):
    return pl.pallas_call(
        merge_kernel,
        out_shape=PIECE_SHAPES,
        in_specs=[SMEM] + [VMEM] * len(arrays),
        out_specs=(VMEM,) * len(PIECES),
        scratch_shapes=[pltpu.VMEM((SLOTS * STRETCH, 2 * HEAD_DIM), jnp.bfloat16)],
        compiler_params=small(MERGE_KIB),
        name="merge_tail",
    )(places, *arrays)


def join(parts):
    return jnp.concatenate(parts, 0)


def wide(value):
    return value.astype(jnp.float32)


def reduce_block(pieces, unit):
    own, other = pieces[:5], pieces[5:]
    arrived = [swap(piece) for piece in other]
    sums = [wide(a) + wide(b) for a, b in zip(own, arrived)]
    mine, up, down, ahead, behind = [sums[0]] + [s.astype(jnp.bfloat16) for s in sums[1:]]
    ahead, behind = shift(ahead, -1, 0), shift(behind, 1, 0)
    up, down = shift(up, 0, -1), shift(down, 0, 1)
    half = up.shape[0]
    mine = mine + wide(ahead) + wide(behind)
    mine = jnp.concatenate([mine[:half] + wide(up) + wide(down), mine[half:]], 0)
    mine_b = mine.astype(jnp.bfloat16)
    back = []
    for i, by_core in enumerate(MEMBERS):
        rows = mine_b[(2 + 2 * i) * unit : (4 + 2 * i) * unit]
        back.append(send(rows, tuple((-dz, -dy) for dz, dy in by_core)))
    opposite = shift(mine_b[unit : 2 * unit], -OPPOSITE[0], -OPPOSITE[1])
    there = sum(wide(b[unit:]) for b in back)
    here = mine[:unit] + wide(opposite) + sum(wide(b[:unit]) for b in back)
    return here + wide(swap(there.astype(jnp.bfloat16)))


def join(parts):
    return jnp.concatenate(parts, 0)


def per_device(query, key, value, grad_out, stretch_order, reach):
    unit = query.shape[0]
    nodes = lax.axis_size("node")
    onward = [(n, (n + 1) % nodes) for n in range(nodes)]
    backward = [((n + 1) % nodes, n) for n in range(nodes)]
    tables = []

    def settle(early, late):
        tables.extend(plan(stretch_order, lax.optimization_barrier((reach, early))[0]))
        late, *tables[:] = lax.optimization_barrier((late, *tables))
        return late

    pieces = gather_block(jnp.concatenate([key, value], axis=1), unit, send, join, settle)
    places, tail_places, facts = tables
    tails = [lax.ppermute(tail, "node", onward) for tail in pick(tail_places, pieces)]
    keys, values = [pieces + [tail, swap(tail)] for tail in tails]

    *carried, block_values, own_tail, other_tail = on_keys(places, facts, query, grad_out, keys)
    tail_values = (wide(own_tail) + wide(swap(other_tail))).astype(jnp.bfloat16)
    carried[0], tail_values = lax.optimization_barrier((carried[0], tail_values))
    tail_values = lax.ppermute(tail_values, "node", backward)
    grad_query, block_keys, own_tail, other_tail = on_values(places, facts, carried, values)
    tail_values, own_tail, other_tail = lax.optimization_barrier((tail_values, own_tail, other_tail))
    tail_keys = (wide(own_tail) + wide(swap(other_tail))).astype(jnp.bfloat16)
    tail_keys = lax.ppermute(tail_keys, "node", backward)
    pieces = merge(tail_places, block_keys, block_values, tail_keys, tail_values)
    sums = reduce_block(pieces, unit).astype(jnp.bfloat16)
    return grad_query, sums[:, :HEAD_DIM], sums[:, HEAD_DIM:]


def solution(mesh):
    rows = P(("node", "local"), None)
    return jax.shard_map(
        per_device,
        mesh=mesh,
        in_specs=(rows, rows, rows, rows, P(), P()),
        out_specs=(rows, rows, rows),
        check_vma=False,
    )
```

time: 165 us -> 128 us (0.78)
  Pallas kernels: 33.8 us -> 19.7 us
  local copies, waits for them, and re-layouts: 14.3 us -> 4.36 us
  waiting for transfers between devices: 61.2 us -> 55.8 us
  starting transfers between devices: 48.7 us -> 45.4 us
  other arithmetic: 4.17 us -> 1.09 us
    pallas_call x3 -> x5, Pallas kernels: 33.8 us -> 19.7 us  [the longest x1 7.24 us: on_keys(): pl.pallas_call(key_kernel, out_shape=(jax.ShapeDtypeStruct((2, WINDOW, CO...]
    unnamed x40 -> x15, local copies, waits for them, and re-layouts: 11.5 us -> 3.68 us
    ppermute x2 -> x4, waiting for transfers between devices: 25.6 us -> 19.6 us  [the longest x1 9.54 us: per_device(): tail_keys = lax.ppermute(tail_keys, 'node', backward)]
    ppermute x30 -> x32, starting transfers between devices: 44.6 us -> 42.4 us  [send(): return lax.ppermute(value, 'local', moves(by_core))]
    ppermute x2 -> x4, starting transfers between devices: 4.06 us -> 3.06 us  [the longest x2 2.24 us: per_device(): lax.ppermute(tail, 'node', onward)]
    ppermute x30 -> x32, waiting for transfers between devices: 35.6 us -> 36.2 us  [send(): return lax.ppermute(value, 'local', moves(by_core))]
  transfers between devices with their start and end apart: 32 -> 36, of which waited for: 16 -> 17; matrix products, arithmetic and copies ran while one was open for 3% -> 1% of each run, Pallas kernels for 0% -> 13%
where the time goes in v2:
time: 128 us; the launch traced here: 127 us
  waiting for transfers between devices  55.8 us (44%)
  starting transfers between devices  45.4 us (35%)
  Pallas kernels  19.7 us (15%)
  local copies, waits for them, and re-layouts  4.36 us (3%)
    ppermute x32, starting transfers between devices, send(): return lax.ppermute(value, 'local', moves(by_core))  42.4 us
    ppermute x32, waiting for transfers between devices, send(): return lax.ppermute(value, 'local', moves(by_core))  36.2 us
    ppermute x1, waiting for transfers between devices, per_device(): tail_keys = lax.ppermute(tail_keys, 'node', backward)  9.54 us
    ppermute x2, waiting for transfers between devices, per_device(): lax.ppermute(tail, 'node', onward)  7.87 us
    pallas_call x1, Pallas kernels, on_keys(): pl.pallas_call(key_kernel, out_shape=(jax.ShapeDtypeStruct((2, WINDOW, CO...  7.24 us
    pallas_call x1, Pallas kernels, on_values(): pl.pallas_call(value_kernel, out_shape=(shape(2 * STRETCH, HEADS * HEAD_D...  6.81 us
    unnamed x15, local copies, waits for them, and re-layouts  3.68 us
    pallas_call x1, Pallas kernels, plan(): pl.pallas_call(plan_kernel, out_shape=tuple((jax.ShapeDtypeStruct((n,), j...  2.82 us
  transfers between devices with their start and end apart: 36, of which 17 were waited for; matrix products, arithmetic and copies ran while one was open for 1% of the time, Pallas kernels for 13%

profile of v2, /device:TPU:6, one launch (start us, length us, event | category | flops | bytes accessed | tf_op | source)
XLA Modules:
  0.0 127.2 jit_solution(9644251601595817759)
XLA Ops:
  0.6 0.8 constant_dynamic-update-slice_fusion.7
  1.4 0.8 constant_dynamic-update-slice_fusion.6
  2.2 0.1 collective-permute-start.1
  2.3 1.2 collective-permute-done.1
  3.5 4.4 %collective-permute-start.2 = (bf16[256,256]{1,0:T(8,128)(2,1)S(1)}, bf16[256,256]{1,0:T(8,128)(2,1)S(1)}, u32[]{:S(2)}, u32[]{:S(2)}) collective-permute-start(bf16[256,256]{1,0:T(8,128)(2,1)S(1)} %pad_maximum_fusion.1), channel_id=1, source_target_pairs={{0,18},{1,51},{2,20},{3,53},{4,22},{5,55},{6,16},{7,49},{8,26},{9,... | collective-permute-start | bytes 393224 | tf_op jit(solution)/shard_map/ppermute | solution.py:47
  7.9 7.7 %collective-permute-start = (bf16[128,256]{1,0:T(8,128)(2,1)S(1)}, bf16[128,256]{1,0:T(8,128)(2,1)S(1)}, u32[]{:S(2)}, u32[]{:S(2)}) collective-permute-start(bf16[128,256]{1,0:T(8,128)(2,1)S(1)} %get-tuple-element.84), channel_id=1, source_target_pairs={{0,36},{1,37},{2,38},{3,39},{4,32},{5,33},{6,34},{7,35},{8,44},{9,... | collective-permute-start | bytes 196616 | tf_op jit(solution)/shard_map/ppermute | solution.py:47
  15.6 0.6 collective-permute-start.4
  16.3 3.8 %collective-permute-start.3 = (bf16[256,256]{1,0:T(8,128)(2,1)S(1)}, bf16[256,256]{1,0:T(8,128)(2,1)S(1)}, u32[]{:S(2)}, u32[]{:S(2)}) collective-permute-start(bf16[256,256]{1,0:T(8,128)(2,1)S(1)} %pad_maximum_fusion.1), channel_id=1, source_target_pairs={{0,54},{1,23},{2,48},{3,17},{4,50},{5,19},{6,52},{7,21},{8,62},{9,... | collective-permute-start | bytes 393224 | tf_op jit(solution)/shard_map/ppermute | solution.py:47
  20.0 0.8 copy-done.2
  20.8 0.7 copy-done.3
  21.5 0.7 copy-done.4
  22.1 2.8 %plan.1 = (s32[66]{0:T(128)S(1)}, s32[16]{0:T(128)S(1)}, s32[5]{0:T(128)S(1)}) custom-call(s32[4,128]{1,0:T(4,128)S(1)} %copy-done.3, s32[4]{0:T(128)S(1)} %copy-done.4, s32[64,128]{1,0:T(8,128)S(1)} %copy-done.2), custom_call_target="tpu_custom_call" | custom-call | tf_op jit(solution)/shard_map/plan/pallas_call | solution.py:154
  25.0 1.4 %collective-permute-done.3 = bf16[256,256]{1,0:T(8,128)(2,1)S(1)} collective-permute-done((bf16[256,256]{1,0:T(8,128)(2,1)S(1)}, bf16[256,256]{1,0:T(8,128)(2,1)S(1)}, u32[]{:S(2)}, u32[]{:S(2)}) %collective-permute-start.3) | collective-permute-done | bytes 131104 | tf_op jit(solution)/shard_map/ppermute | solution.py:47
  26.4 0.6 collective-permute-start.8
  27.1 1.5 %collective-permute-start.7 = (bf16[1024,256]{1,0:T(8,128)(2,1)S(1)}, bf16[1024,256]{1,0:T(8,128)(2,1)S(1)}, u32[]{:S(2)}, u32[]{:S(2)}) collective-permute-start(bf16[1024,256]{1,0:T(8,128)(2,1)S(1)} %constant_dynamic-update-slice_fusion.2.refs_0_), channel_id=1, source_target_pairs={{0,8},{1,9},{2,10},{3,11},{4,12},{5,13},{6,14},{7,15},{8,16},{9,17... | collective-permute-start | bytes 1572872 | tf_op jit(solution)/shard_map/ppermute | solution.py:47
  28.6 2.8 %collective-permute-start.6 = (bf16[512,256]{1,0:T(8,128)(2,1)S(1)}, bf16[512,256]{1,0:T(8,128)(2,1)S(1)}, u32[]{:S(2)}, u32[]{:S(2)}) collective-permute-start(bf16[512,256]{1,0:T(8,128)(2,1)S(1)} %pad_maximum_fusion), channel_id=1, source_target_pairs={{0,6},{1,7},{2,0},{3,1},{4,2},{5,3},{6,4},{7,5},{8,14},{9,15},{10,... | collective-permute-start | bytes 786440 | tf_op jit(solution)/shard_map/ppermute | solution.py:47
  31.4 8.9 %collective-permute-done.8.refs_4_ = bf16[1024,256]{1,0:T(8,128)(2,1)S(1)} collective-permute-done((bf16[1024,256]{1,0:T(8,128)(2,1)S(1)}, bf16[1024,256]{1,0:T(8,128)(2,1)S(1)}, u32[]{:S(2)}, u32[]{:S(2)}) %collective-permute-start.8) | collective-permute-done | bytes 524320 | tf_op jit(solution)/shard_map/ppermute | solution.py:47
  40.3 2.3 %collective-permute-done.7.refs_3_ = bf16[1024,256]{1,0:T(8,128)(2,1)S(1)} collective-permute-done((bf16[1024,256]{1,0:T(8,128)(2,1)S(1)}, bf16[1024,256]{1,0:T(8,128)(2,1)S(1)}, u32[]{:S(2)}, u32[]{:S(2)}) %collective-permute-start.7) | collective-permute-done | bytes 524320 | tf_op jit(solution)/shard_map/ppermute | solution.py:47
  42.6 0.5 collective-permute-start.11
  43.1 0.1 collective-permute-start.10
  43.2 1.7 %collective-permute-done.11.refs_7_ = bf16[512,256]{1,0:T(8,128)(2,1)S(1)} collective-permute-done((bf16[512,256]{1,0:T(8,128)(2,1)S(1)}, bf16[512,256]{1,0:T(8,128)(2,1)S(1)}, u32[]{:S(2)}, u32[]{:S(2)}) %collective-permute-start.11) | collective-permute-done | bytes 262176 | tf_op jit(solution)/shard_map/ppermute | solution.py:47
  44.9 0.4 collective-permute-done.10.refs_6_
  45.3 1.0 pick_tail.1
  46.2 0.6 collective-permute-start.14
  46.8 7.9 %collective-permute-done.14.refs_10_ = bf16[1024,128]{1,0:T(8,128)(2,1)S(1)} collective-permute-done((bf16[1024,128]{1,0:T(8,128)(2,1)S(1)}, bf16[1024,128]{1,0:T(8,128)(2,1)S(1)}, u32[]{:S(2)}, u32[]{:S(2)}) %collective-permute-start.14) | collective-permute-done | bytes 262176 | tf_op jit(solution)/shard_map/ppermute | solution.py:446
  54.7 1.7 %collective-permute-start.17 = (bf16[1024,128]{1,0:T(8,128)(2,1)S(1)}, bf16[1024,128]{1,0:T(8,128)(2,1)S(1)}, u32[]{:S(2)}, u32[]{:S(2)}) collective-permute-start(bf16[1024,128]{1,0:T(8,128)(2,1)S(1)} %get-tuple-element.55), channel_id=1, source_target_pairs={{0,64},{64,128},{128,192},{192,0},{1,65},{65,129},{129,193},{193,1... | collective-permute-start | bytes 786440 | tf_op jit(solution)/shard_map/ppermute | solution.py:446
  56.4 7.2 %on_keys.1 = (bf16[2,2112,512]{2,1,0:T(8,128)(2,1)S(1)}, bf16[2,2112,128]{2,1,0:T(8,128)(2,1)S(1)}, bf16[2,512,128]{2,1,0:T(8,128)(2,1)S(1)}, bf16[2,512,128]{2,...) custom-call(s32[66]{0:T(128)S(1)} %get-tuple-element.43.places, ...), custom_call_target="tpu_custom_call" | custom-call | tf_op jit(solution)/shard_map/on_keys/pallas_call | solution.py:331
  63.6 0.3 collective-permute-start.16
  63.9 0.3 collective-permute-start.18
  64.2 1.0 collective-permute-done.16
  65.2 0.1 add_convert_fusion.5
  65.3 0.7 collective-permute-start.19
  66.1 6.8 %on_values.1 = (bf16[128,1024]{1,0:T(8,128)(2,1)}, bf16[8192,128]{1,0:T(8,128)(2,1)S(1)}, bf16[1024,128]{1,0:T(8,128)(2,1)S(1)}, bf16[1024,128]{1,0:T(8,128)(2,1)S(1)}) custom-call(s32[66]{0:T(128)S(1)} %get-tuple-element.43.places, s32[5]{0:T(128)S(1)} %get-tuple-element.44.facts, bf16[2,2112,512]{2,1,0:T(8,128)(2,1)S(1)} %get-tuple-element.51.prob_in, ...), custom_call_target="tpu_custom_call" | custom-call | flops 3321888768 | bytes 12582912 | tf_op jit(solution)/shard_map/on_values/pallas_call | solution.py:354
  72.9 2.2 %collective-permute-done.19.tail_values = bf16[1024,128]{1,0:T(8,128)(2,1)S(1)} collective-permute-done((bf16[1024,128]{1,0:T(8,128)(2,1)S(1)}, bf16[1024,128]{1,0:T(8,128)(2,1)S(1)}, u32[]{:S(2)}, u32[]{:S(2)}) %collective-permute-start.19) | collective-permute-done | bytes 262176 | tf_op jit(solution)/shard_map/ppermute | solution.py:452
  75.0 1.5 %collective-permute-done.20 = bf16[1024,128]{1,0:T(8,128)(2,1)S(1)} collective-permute-done((bf16[1024,128]{1,0:T(8,128)(2,1)S(1)}, bf16[1024,128]{1,0:T(8,128)(2,1)S(1)}, u32[]{:S(2)}, u32[]{:S(2)}) %collective-permute-start.20) | collective-permute-done | bytes 262176 | tf_op jit(solution)/shard_map/ppermute | solution.py:47
  76.6 0.1 add_convert_fusion.4
  76.7 0.1 collective-permute-start.21
  76.7 9.5 %collective-permute-done.21.tail_keys = bf16[1024,128]{1,0:T(8,128)(2,1)S(1)} collective-permute-done((bf16[1024,128]{1,0:T(8,128)(2,1)S(1)}, bf16[1024,128]{1,0:T(8,128)(2,1)S(1)}, u32[]{:S(2)}, u32[]{:S(2)}) %collective-permute-start.21) | collective-permute-done | bytes 262176 | tf_op jit(solution)/shard_map/ppermute | solution.py:456
  86.3 1.8 %merge_tail.1 = (bf16[1024,256]{1,0:T(8,128)(2,1)S(1)}, bf16[512,256]{1,0:T(8,128)(2,1)S(1)}, bf16[512,256]{1,0:T(8,128)(2,1)S(1)}, bf16[1024,256]{1,0:T(8,128)(...) custom-call(s32[16]{0:T(128)S(1)} %get-tuple-element.46.places, ...), custom_call_target="tpu_custom_call" | custom-call | tf_op jit(solution)/shard_map/merge_tail/pallas_call | solution.py:388
  88.1 0.1 collective-permute-start.23
  88.2 0.5 collective-permute-start.25
  88.7 0.1 collective-permute-start.27
  88.8 0.4 collective-permute-start.22
  89.2 0.9 collective-permute-done.23
  90.1 0.1 add_convert_fusion.1
  90.3 1.1 collective-permute-start.24
  91.4 0.1 add_convert_fusion
  91.5 1.1 collective-permute-start.26
  92.7 2.8 %collective-permute-start.28 = (bf16[512,256]{1,0:T(8,128)(2,1)S(1)}, bf16[512,256]{1,0:T(8,128)(2,1)S(1)}, u32[]{:S(2)}, u32[]{:S(2)}) collective-permute-start(bf16[512,256]{1,0:T(8,128)(2,1)S(1)} %add_convert_fusion.3), channel_id=1, source_target_pairs={{0,6},{1,7},{2,0},{3,1},{4,2},{5,3},{6,4},{7,5},{8,14},{9,15},{10,... | collective-permute-start | bytes 786440 | tf_op jit(solution)/shard_map/ppermute | solution.py:47
  95.5 0.1 add_convert_fusion.2
  95.6 0.1 collective-permute-start.30
  95.7 8.6 %collective-permute-done.24 = bf16[1024,256]{1,0:T(8,128)(2,1)S(1)} collective-permute-done((bf16[1024,256]{1,0:T(8,128)(2,1)S(1)}, bf16[1024,256]{1,0:T(8,128)(2,1)S(1)}, u32[]{:S(2)}, u32[]{:S(2)}) %collective-permute-start.24) | collective-permute-done | bytes 524320 | tf_op jit(solution)/shard_map/ppermute | solution.py:47
  104.3 2.2 %collective-permute-done.26 = bf16[1024,256]{1,0:T(8,128)(2,1)S(1)} collective-permute-done((bf16[1024,256]{1,0:T(8,128)(2,1)S(1)}, bf16[1024,256]{1,0:T(8,128)(2,1)S(1)}, u32[]{:S(2)}, u32[]{:S(2)}) %collective-permute-start.26) | collective-permute-done | bytes 524320 | tf_op jit(solution)/shard_map/ppermute | solution.py:47
  106.5 0.3 fusion.6
  106.8 0.3 collective-permute-start.33
  107.1 3.0 %collective-permute-start.34 = (bf16[256,256]{1,0:T(8,128)(2,1)S(1)}, bf16[256,256]{1,0:T(8,128)(2,1)S(1)}, u32[]{:S(2)}, u32[]{:S(2)}) collective-permute-start(bf16[256,256]{1,0:T(8,128)(2,1)S(1)} %get-tuple-element.80), channel_id=1, source_target_pairs={{0,4},{1,33},{2,6},{3,35},{4,0},{5,37},{6,2},{7,39},{8,12},{9,41},... | collective-permute-start | bytes 393224 | tf_op jit(solution)/shard_map/ppermute | solution.py:47
  110.1 0.1 fusion.4
  110.2 5.1 %collective-permute-start.32 = (bf16[256,256]{1,0:T(8,128)(2,1)S(1)}, bf16[256,256]{1,0:T(8,128)(2,1)S(1)}, u32[]{:S(2)}, u32[]{:S(2)}) collective-permute-start(bf16[256,256]{1,0:T(8,128)(2,1)S(1)} %slice.70), channel_id=1, source_target_pairs={{0,54},{1,23},{2,48},{3,17},{4,50},{5,19},{6,52},{7,21},{8,62},{9,... | collective-permute-start | bytes 393224 | tf_op jit(solution)/shard_map/ppermute | solution.py:47
  115.4 3.1 %collective-permute-start.31 = (bf16[128,256]{1,0:T(8,128)(2,1)S(1)}, bf16[128,256]{1,0:T(8,128)(2,1)S(1)}, u32[]{:S(2)}, u32[]{:S(2)}) collective-permute-start(bf16[128,256]{1,0:T(8,128)(2,1)S(1)} %slice.69), channel_id=1, source_target_pairs={{0,36},{1,37},{2,38},{3,39},{4,32},{5,33},{6,34},{7,35},{8,44},{9,... | collective-permute-start | bytes 196616 | tf_op jit(solution)/shard_map/ppermute | solution.py:47
  118.5 2.5 %collective-permute-done.33 = bf16[256,256]{1,0:T(8,128)(2,1)S(1)} collective-permute-done((bf16[256,256]{1,0:T(8,128)(2,1)S(1)}, bf16[256,256]{1,0:T(8,128)(2,1)S(1)}, u32[]{:S(2)}, u32[]{:S(2)}) %collective-permute-start.33) | collective-permute-done | bytes 131104 | tf_op jit(solution)/shard_map/ppermute | solution.py:47
  121.0 1.1 collective-permute-done.32
  122.1 1.9 %collective-permute-start.35 = (bf16[128,256]{1,0:T(8,128)(2,1)S(1)}, bf16[128,256]{1,0:T(8,128)(2,1)S(1)}, u32[]{:S(2)}, u32[]{:S(2)}) collective-permute-start(bf16[128,256]{1,0:T(8,128)(2,1)S(1)} %add_convert_fusion.6), channel_id=1, source_target_pairs={{0,1},{1,0},{2,3},{3,2},{4,5},{5,4},{6,7},{7,6},{8,9},{9,8},{10,11... | collective-permute-start | bytes 196616 | tf_op jit(solution)/shard_map/ppermute | solution.py:47
  124.0 2.5 %collective-permute-done.31 = bf16[128,256]{1,0:T(8,128)(2,1)S(1)} collective-permute-done((bf16[128,256]{1,0:T(8,128)(2,1)S(1)}, bf16[128,256]{1,0:T(8,128)(2,1)S(1)}, u32[]{:S(2)}, u32[]{:S(2)}) %collective-permute-start.31) | collective-permute-done | bytes 65568 | tf_op jit(solution)/shard_map/ppermute | solution.py:47
  126.6 0.6 fusion.8
  (45 shorter events, 0.3 us)
Async XLA Ops:
  2.2 1.3 %collective-permute-start.1 = (bf16[128,256]{1,0:T(8,128)(2,1)S(1)}, bf16[128,256]{1,0:T(8,128)(2,1)S(1)}, u32[]{:S(2)}, u32[]{:S(2)}) collective-permute-start(bf16[128,256]{1,0:T(8,128)(2,1)S(1)} %get-tuple-element.84), channel_id=1, source_target_pairs={{0,1},{1,0},{2,3},{3,2},{4,5},{5,4},{6,7},{7,6},{8,9},{9,8},{10,11... | collective-permute-start | bytes 196616 | tf_op jit(solution)/shard_map/ppermute | solution.py:47
  3.5 16.5 %collective-permute-start.2 = (bf16[256,256]{1,0:T(8,128)(2,1)S(1)}, bf16[256,256]{1,0:T(8,128)(2,1)S(1)}, u32[]{:S(2)}, u32[]{:S(2)}) collective-permute-start(bf16[256,256]{1,0:T(8,128)(2,1)S(1)} %pad_maximum_fusion.1), channel_id=1, source_target_pairs={{0,18},{1,51},{2,20},{3,53},{4,22},{5,55},{6,16},{7,49},{8,26},{9,... | collective-permute-start | bytes 393224 | tf_op jit(solution)/shard_map/ppermute | solution.py:47
  7.9 17.1 %collective-permute-start = (bf16[128,256]{1,0:T(8,128)(2,1)S(1)}, bf16[128,256]{1,0:T(8,128)(2,1)S(1)}, u32[]{:S(2)}, u32[]{:S(2)}) collective-permute-start(bf16[128,256]{1,0:T(8,128)(2,1)S(1)} %get-tuple-element.84), channel_id=1, source_target_pairs={{0,36},{1,37},{2,38},{3,39},{4,32},{5,33},{6,34},{7,35},{8,44},{9,... | collective-permute-start | bytes 196616 | tf_op jit(solution)/shard_map/ppermute | solution.py:47
  15.6 10.8 %collective-permute-start.4 = (bf16[256,256]{1,0:T(8,128)(2,1)S(1)}, bf16[256,256]{1,0:T(8,128)(2,1)S(1)}, u32[]{:S(2)}, u32[]{:S(2)}) collective-permute-start(bf16[256,256]{1,0:T(8,128)(2,1)S(1)} %pad_maximum_fusion.1), channel_id=1, source_target_pairs={{0,4},{1,33},{2,6},{3,35},{4,0},{5,37},{6,2},{7,39},{8,12},{9,41},... | collective-permute-start | bytes 393224 | tf_op jit(solution)/shard_map/ppermute | solution.py:47
  16.3 10.1 %collective-permute-start.3 = (bf16[256,256]{1,0:T(8,128)(2,1)S(1)}, bf16[256,256]{1,0:T(8,128)(2,1)S(1)}, u32[]{:S(2)}, u32[]{:S(2)}) collective-permute-start(bf16[256,256]{1,0:T(8,128)(2,1)S(1)} %pad_maximum_fusion.1), channel_id=1, source_target_pairs={{0,54},{1,23},{2,48},{3,17},{4,50},{5,19},{6,52},{7,21},{8,62},{9,... | collective-permute-start | bytes 393224 | tf_op jit(solution)/shard_map/ppermute | solution.py:47
  20.0 0.8 copy-start.2
  20.8 0.7 copy-start.3
  21.5 0.7 copy-start.4
  26.4 13.9 %collective-permute-start.8 = (bf16[1024,256]{1,0:T(8,128)(2,1)S(1)}, bf16[1024,256]{1,0:T(8,128)(2,1)S(1)}, u32[]{:S(2)}, u32[]{:S(2)}) collective-permute-start(bf16[1024,256]{1,0:T(8,128)(2,1)S(1)} %constant_dynamic-update-slice_fusion.2.refs_0_), channel_id=1, source_target_pairs={{0,56},{1,57},{2,58},{3,59},{4,60},{5,61},{6,62},{7,63},{8,0},{9,1... | collective-permute-start | bytes 1572872 | tf_op jit(solution)/shard_map/ppermute | solution.py:47
  27.1 15.5 %collective-permute-start.7 = (bf16[1024,256]{1,0:T(8,128)(2,1)S(1)}, bf16[1024,256]{1,0:T(8,128)(2,1)S(1)}, u32[]{:S(2)}, u32[]{:S(2)}) collective-permute-start(bf16[1024,256]{1,0:T(8,128)(2,1)S(1)} %constant_dynamic-update-slice_fusion.2.refs_0_), channel_id=1, source_target_pairs={{0,8},{1,9},{2,10},{3,11},{4,12},{5,13},{6,14},{7,15},{8,16},{9,17... | collective-permute-start | bytes 1572872 | tf_op jit(solution)/shard_map/ppermute | solution.py:47
  28.5 27.8 %copy-start = (bf16[128,1024]{1,0:T(8,128)(2,1)S(1)}, bf16[128,1024]{1,0:T(8,128)(2,1)}, u32[]{:S(2)}) copy-start(bf16[128,1024]{1,0:T(8,128)(2,1)} %query.1) | copy-start | bytes 786436
  28.6 27.8 %copy-start.1 = (bf16[128,1024]{1,0:T(8,128)(2,1)S(1)}, bf16[128,1024]{1,0:T(8,128)(2,1)}, u32[]{:S(2)}) copy-start(bf16[128,1024]{1,0:T(8,128)(2,1)} %grad_out.1) | copy-start | bytes 786436
  28.6 14.0 %collective-permute-start.6 = (bf16[512,256]{1,0:T(8,128)(2,1)S(1)}, bf16[512,256]{1,0:T(8,128)(2,1)S(1)}, u32[]{:S(2)}, u32[]{:S(2)}) collective-permute-start(bf16[512,256]{1,0:T(8,128)(2,1)S(1)} %pad_maximum_fusion), channel_id=1, source_target_pairs={{0,6},{1,7},{2,0},{3,1},{4,2},{5,3},{6,4},{7,5},{8,14},{9,15},{10,... | collective-permute-start | bytes 786440 | tf_op jit(solution)/shard_map/ppermute | solution.py:47
  31.4 11.7 %collective-permute-start.5 = (bf16[512,256]{1,0:T(8,128)(2,1)S(1)}, bf16[512,256]{1,0:T(8,128)(2,1)S(1)}, u32[]{:S(2)}, u32[]{:S(2)}) collective-permute-start(bf16[512,256]{1,0:T(8,128)(2,1)S(1)} %pad_maximum_fusion), channel_id=1, source_target_pairs={{0,2},{1,3},{2,4},{3,5},{4,6},{5,7},{6,0},{7,1},{8,10},{9,11},{10,... | collective-permute-start | bytes 786440 | tf_op jit(solution)/shard_map/ppermute | solution.py:47
  31.4 11.8 %collective-permute-start.9 = (bf16[1024,256]{1,0:T(8,128)(2,1)S(1)}, bf16[1024,256]{1,0:T(8,128)(2,1)S(1)}, u32[]{:S(2)}, u32[]{:S(2)}) collective-permute-start(bf16[1024,256]{1,0:T(8,128)(2,1)S(1)} %constant_dynamic-update-slice_fusion.2.refs_0_), channel_id=1, source_target_pairs={{0,1},{1,0},{2,3},{3,2},{4,5},{5,4},{6,7},{7,6},{8,9},{9,8},{10,11... | collective-permute-start | bytes 1572872 | tf_op jit(solution)/shard_map/ppermute | solution.py:47
  40.3 5.0 %collective-permute-start.13 = (bf16[1024,256]{1,0:T(8,128)(2,1)S(1)}, bf16[1024,256]{1,0:T(8,128)(2,1)S(1)}, u32[]{:S(2)}, u32[]{:S(2)}) collective-permute-start(bf16[1024,256]{1,0:T(8,128)(2,1)S(1)} %collective-permute-done.8.refs_4_), channel_id=1, source_target_pairs={{0,1},{1,0},{2,3},{3,2},{4,5},{5,4},{6,7},{7,6},{8,9},{9,8},{10,11... | collective-permute-start | bytes 1572872 | tf_op jit(solution)/shard_map/ppermute | solution.py:47
  42.6 2.7 %collective-permute-start.12 = (bf16[1024,256]{1,0:T(8,128)(2,1)S(1)}, bf16[1024,256]{1,0:T(8,128)(2,1)S(1)}, u32[]{:S(2)}, u32[]{:S(2)}) collective-permute-start(bf16[1024,256]{1,0:T(8,128)(2,1)S(1)} %collective-permute-done.7.refs_3_), channel_id=1, source_target_pairs={{0,1},{1,0},{2,3},{3,2},{4,5},{5,4},{6,7},{7,6},{8,9},{9,8},{10,11... | collective-permute-start | bytes 1572872 | tf_op jit(solution)/shard_map/ppermute | solution.py:47
  42.6 2.3 %collective-permute-start.11 = (bf16[512,256]{1,0:T(8,128)(2,1)S(1)}, bf16[512,256]{1,0:T(8,128)(2,1)S(1)}, u32[]{:S(2)}, u32[]{:S(2)}) collective-permute-start(bf16[512,256]{1,0:T(8,128)(2,1)S(1)} %collective-permute-done.6.refs_2_), channel_id=1, source_target_pairs={{0,1},{1,0},{2,3},{3,2},{4,5},{5,4},{6,7},{7,6},{8,9},{9,8},{10,11... | collective-permute-start | bytes 786440 | tf_op jit(solution)/shard_map/ppermute | solution.py:47
  43.1 2.1 %collective-permute-start.10 = (bf16[512,256]{1,0:T(8,128)(2,1)S(1)}, bf16[512,256]{1,0:T(8,128)(2,1)S(1)}, u32[]{:S(2)}, u32[]{:S(2)}) collective-permute-start(bf16[512,256]{1,0:T(8,128)(2,1)S(1)} %collective-permute-done.5.refs_1_), channel_id=1, source_target_pairs={{0,1},{1,0},{2,3},{3,2},{4,5},{5,4},{6,7},{7,6},{8,9},{9,8},{10,11... | collective-permute-start | bytes 786440 | tf_op jit(solution)/shard_map/ppermute | solution.py:47
  46.2 8.4 %collective-permute-start.14 = (bf16[1024,128]{1,0:T(8,128)(2,1)S(1)}, bf16[1024,128]{1,0:T(8,128)(2,1)S(1)}, u32[]{:S(2)}, u32[]{:S(2)}) collective-permute-start(bf16[1024,128]{1,0:T(8,128)(2,1)S(1)} %get-tuple-element.47), channel_id=1, source_target_pairs={{0,64},{64,128},{128,192},{192,0},{1,65},{65,129},{129,193},{193,1... | collective-permute-start | bytes 786440 | tf_op jit(solution)/shard_map/ppermute | solution.py:446
  54.7 1.7 %collective-permute-start.15 = (bf16[1024,128]{1,0:T(8,128)(2,1)S(1)}, bf16[1024,128]{1,0:T(8,128)(2,1)S(1)}, u32[]{:S(2)}, u32[]{:S(2)}) collective-permute-start(bf16[1024,128]{1,0:T(8,128)(2,1)S(1)} %collective-permute-done.14.refs_10_), channel_id=1, source_target_pairs={{0,1},{1,0},{2,3},{3,2},{4,5},{5,4},{6,7},{7,6},{8,9},{9,8},{10,11... | collective-permute-start | bytes 786440 | tf_op jit(solution)/shard_map/ppermute | solution.py:47
  54.7 9.3 %collective-permute-start.17 = (bf16[1024,128]{1,0:T(8,128)(2,1)S(1)}, bf16[1024,128]{1,0:T(8,128)(2,1)S(1)}, u32[]{:S(2)}, u32[]{:S(2)}) collective-permute-start(bf16[1024,128]{1,0:T(8,128)(2,1)S(1)} %get-tuple-element.55), channel_id=1, source_target_pairs={{0,64},{64,128},{128,192},{192,0},{1,65},{65,129},{129,193},{193,1... | collective-permute-start | bytes 786440 | tf_op jit(solution)/shard_map/ppermute | solution.py:446
  63.6 1.6 %collective-permute-start.16 = (bf16[1024,128]{1,0:T(8,128)(2,1)S(1)}, bf16[1024,128]{1,0:T(8,128)(2,1)S(1)}, u32[]{:S(2)}, u32[]{:S(2)}) collective-permute-start(bf16[1024,128]{1,0:T(8,128)(2,1)S(1)} %get-tuple-element.50), channel_id=1, source_target_pairs={{0,1},{1,0},{2,3},{3,2},{4,5},{5,4},{6,7},{7,6},{8,9},{9,8},{10,11... | collective-permute-start | bytes 786440 | tf_op jit(solution)/shard_map/ppermute | solution.py:47
  63.9 2.1 %collective-permute-start.18 = (bf16[1024,128]{1,0:T(8,128)(2,1)S(1)}, bf16[1024,128]{1,0:T(8,128)(2,1)S(1)}, u32[]{:S(2)}, u32[]{:S(2)}) collective-permute-start(bf16[1024,128]{1,0:T(8,128)(2,1)S(1)} %collective-permute-done.17.refs_10_), channel_id=1, source_target_pairs={{0,1},{1,0},{2,3},{3,2},{4,5},{5,4},{6,7},{7,6},{8,9},{9,8},{10,11... | collective-permute-start | bytes 786440 | tf_op jit(solution)/shard_map/ppermute | solution.py:47
  65.3 9.7 %collective-permute-start.19 = (bf16[1024,128]{1,0:T(8,128)(2,1)S(1)}, bf16[1024,128]{1,0:T(8,128)(2,1)S(1)}, u32[]{:S(2)}, u32[]{:S(2)}) collective-permute-start(bf16[1024,128]{1,0:T(8,128)(2,1)S(1)} %add_convert_fusion.5), channel_id=1, source_target_pairs={{64,0},{128,64},{192,128},{0,192},{65,1},{129,65},{193,129},{1,193... | collective-permute-start | bytes 786440 | tf_op jit(solution)/shard_map/ppermute | solution.py:452
  75.0 1.5 %collective-permute-start.20 = (bf16[1024,128]{1,0:T(8,128)(2,1)S(1)}, bf16[1024,128]{1,0:T(8,128)(2,1)S(1)}, u32[]{:S(2)}, u32[]{:S(2)}) collective-permute-start(bf16[1024,128]{1,0:T(8,128)(2,1)S(1)} %get-tuple-element.63), channel_id=1, source_target_pairs={{0,1},{1,0},{2,3},{3,2},{4,5},{5,4},{6,7},{7,6},{8,9},{9,8},{10,11... | collective-permute-start | bytes 786440 | tf_op jit(solution)/shard_map/ppermute | solution.py:47
  76.7 9.6 %collective-permute-start.21 = (bf16[1024,128]{1,0:T(8,128)(2,1)S(1)}, bf16[1024,128]{1,0:T(8,128)(2,1)S(1)}, u32[]{:S(2)}, u32[]{:S(2)}) collective-permute-start(bf16[1024,128]{1,0:T(8,128)(2,1)S(1)} %add_convert_fusion.4), channel_id=1, source_target_pairs={{64,0},{128,64},{192,128},{0,192},{65,1},{129,65},{193,129},{1,193... | collective-permute-start | bytes 786440 | tf_op jit(solution)/shard_map/ppermute | solution.py:456
  88.1 2.0 %collective-permute-start.23 = (bf16[1024,256]{1,0:T(8,128)(2,1)S(1)}, bf16[1024,256]{1,0:T(8,128)(2,1)S(1)}, u32[]{:S(2)}, u32[]{:S(2)}) collective-permute-start(bf16[1024,256]{1,0:T(8,128)(2,1)S(1)} %get-tuple-element.68), channel_id=1, source_target_pairs={{0,1},{1,0},{2,3},{3,2},{4,5},{5,4},{6,7},{7,6},{8,9},{9,8},{10,11... | collective-permute-start | bytes 1572872 | tf_op jit(solution)/shard_map/ppermute | solution.py:47
  88.2 3.2 %collective-permute-start.25 = (bf16[1024,256]{1,0:T(8,128)(2,1)S(1)}, bf16[1024,256]{1,0:T(8,128)(2,1)S(1)}, u32[]{:S(2)}, u32[]{:S(2)}) collective-permute-start(bf16[1024,256]{1,0:T(8,128)(2,1)S(1)} %get-tuple-element.70), channel_id=1, source_target_pairs={{0,1},{1,0},{2,3},{3,2},{4,5},{5,4},{6,7},{7,6},{8,9},{9,8},{10,11... | collective-permute-start | bytes 1572872 | tf_op jit(solution)/shard_map/ppermute | solution.py:47
  88.7 3.9 %collective-permute-start.27 = (bf16[512,256]{1,0:T(8,128)(2,1)S(1)}, bf16[512,256]{1,0:T(8,128)(2,1)S(1)}, u32[]{:S(2)}, u32[]{:S(2)}) collective-permute-start(bf16[512,256]{1,0:T(8,128)(2,1)S(1)} %get-tuple-element.72), channel_id=1, source_target_pairs={{0,1},{1,0},{2,3},{3,2},{4,5},{5,4},{6,7},{7,6},{8,9},{9,8},{10,11... | collective-permute-start | bytes 786440 | tf_op jit(solution)/shard_map/ppermute | solution.py:47
  88.8 6.9 %collective-permute-start.22 = (bf16[1024,256]{1,0:T(8,128)(2,1)S(1)}, bf16[1024,256]{1,0:T(8,128)(2,1)S(1)}, u32[]{:S(2)}, u32[]{:S(2)}) collective-permute-start(bf16[1024,256]{1,0:T(8,128)(2,1)S(1)} %get-tuple-element.66), channel_id=1, source_target_pairs={{0,1},{1,0},{2,3},{3,2},{4,5},{5,4},{6,7},{7,6},{8,9},{9,8},{10,11... | collective-permute-start | bytes 1572872 | tf_op jit(solution)/shard_map/ppermute | solution.py:47
  90.3 14.0 %collective-permute-start.24 = (bf16[1024,256]{1,0:T(8,128)(2,1)S(1)}, bf16[1024,256]{1,0:T(8,128)(2,1)S(1)}, u32[]{:S(2)}, u32[]{:S(2)}) collective-permute-start(bf16[1024,256]{1,0:T(8,128)(2,1)S(1)} %add_convert_fusion.1), channel_id=1, source_target_pairs={{0,56},{1,57},{2,58},{3,59},{4,60},{5,61},{6,62},{7,63},{8,0},{9,1... | collective-permute-start | bytes 1572872 | tf_op jit(solution)/shard_map/ppermute | solution.py:47
  91.5 15.0 %collective-permute-start.26 = (bf16[1024,256]{1,0:T(8,128)(2,1)S(1)}, bf16[1024,256]{1,0:T(8,128)(2,1)S(1)}, u32[]{:S(2)}, u32[]{:S(2)}) collective-permute-start(bf16[1024,256]{1,0:T(8,128)(2,1)S(1)} %add_convert_fusion), channel_id=1, source_target_pairs={{0,8},{1,9},{2,10},{3,11},{4,12},{5,13},{6,14},{7,15},{8,16},{9,17... | collective-permute-start | bytes 1572872 | tf_op jit(solution)/shard_map/ppermute | solution.py:47
  92.6 2.9 %collective-permute-start.29 = (bf16[512,256]{1,0:T(8,128)(2,1)S(1)}, bf16[512,256]{1,0:T(8,128)(2,1)S(1)}, u32[]{:S(2)}, u32[]{:S(2)}) collective-permute-start(bf16[512,256]{1,0:T(8,128)(2,1)S(1)} %get-tuple-element.74), channel_id=1, source_target_pairs={{0,1},{1,0},{2,3},{3,2},{4,5},{5,4},{6,7},{7,6},{8,9},{9,8},{10,11... | collective-permute-start | bytes 786440 | tf_op jit(solution)/shard_map/ppermute | solution.py:47
  92.7 17.4 %collective-permute-start.28 = (bf16[512,256]{1,0:T(8,128)(2,1)S(1)}, bf16[512,256]{1,0:T(8,128)(2,1)S(1)}, u32[]{:S(2)}, u32[]{:S(2)}) collective-permute-start(bf16[512,256]{1,0:T(8,128)(2,1)S(1)} %add_convert_fusion.3), channel_id=1, source_target_pairs={{0,6},{1,7},{2,0},{3,1},{4,2},{5,3},{6,4},{7,5},{8,14},{9,15},{10,... | collective-permute-start | bytes 786440 | tf_op jit(solution)/shard_map/ppermute | solution.py:47
  95.6 14.5 %collective-permute-start.30 = (bf16[512,256]{1,0:T(8,128)(2,1)S(1)}, bf16[512,256]{1,0:T(8,128)(2,1)S(1)}, u32[]{:S(2)}, u32[]{:S(2)}) collective-permute-start(bf16[512,256]{1,0:T(8,128)(2,1)S(1)} %add_convert_fusion.2), channel_id=1, source_target_pairs={{0,2},{1,3},{2,4},{3,5},{4,6},{5,7},{6,0},{7,1},{8,10},{9,11},{10,... | collective-permute-start | bytes 786440 | tf_op jit(solution)/shard_map/ppermute | solution.py:47
  106.8 14.2 %collective-permute-start.33 = (bf16[256,256]{1,0:T(8,128)(2,1)S(1)}, bf16[256,256]{1,0:T(8,128)(2,1)S(1)}, u32[]{:S(2)}, u32[]{:S(2)}) collective-permute-start(bf16[256,256]{1,0:T(8,128)(2,1)S(1)} %get-tuple-element.79), channel_id=1, source_target_pairs={{0,18},{1,51},{2,20},{3,53},{4,22},{5,55},{6,16},{7,49},{8,26},{9,... | collective-permute-start | bytes 393224 | tf_op jit(solution)/shard_map/ppermute | solution.py:47
  107.1 13.9 %collective-permute-start.34 = (bf16[256,256]{1,0:T(8,128)(2,1)S(1)}, bf16[256,256]{1,0:T(8,128)(2,1)S(1)}, u32[]{:S(2)}, u32[]{:S(2)}) collective-permute-start(bf16[256,256]{1,0:T(8,128)(2,1)S(1)} %get-tuple-element.80), channel_id=1, source_target_pairs={{0,4},{1,33},{2,6},{3,35},{4,0},{5,37},{6,2},{7,39},{8,12},{9,41},... | collective-permute-start | bytes 393224 | tf_op jit(solution)/shard_map/ppermute | solution.py:47
  110.2 11.8 %collective-permute-start.32 = (bf16[256,256]{1,0:T(8,128)(2,1)S(1)}, bf16[256,256]{1,0:T(8,128)(2,1)S(1)}, u32[]{:S(2)}, u32[]{:S(2)}) collective-permute-start(bf16[256,256]{1,0:T(8,128)(2,1)S(1)} %slice.70), channel_id=1, source_target_pairs={{0,54},{1,23},{2,48},{3,17},{4,50},{5,19},{6,52},{7,21},{8,62},{9,... | collective-permute-start | bytes 393224 | tf_op jit(solution)/shard_map/ppermute | solution.py:47
  115.4 11.1 %collective-permute-start.31 = (bf16[128,256]{1,0:T(8,128)(2,1)S(1)}, bf16[128,256]{1,0:T(8,128)(2,1)S(1)}, u32[]{:S(2)}, u32[]{:S(2)}) collective-permute-start(bf16[128,256]{1,0:T(8,128)(2,1)S(1)} %slice.69), channel_id=1, source_target_pairs={{0,36},{1,37},{2,38},{3,39},{4,32},{5,33},{6,34},{7,35},{8,44},{9,... | collective-permute-start | bytes 196616 | tf_op jit(solution)/shard_map/ppermute | solution.py:47
  122.1 4.4 %collective-permute-start.35 = (bf16[128,256]{1,0:T(8,128)(2,1)S(1)}, bf16[128,256]{1,0:T(8,128)(2,1)S(1)}, u32[]{:S(2)}, u32[]{:S(2)}) collective-permute-start(bf16[128,256]{1,0:T(8,128)(2,1)S(1)} %add_convert_fusion.6), channel_id=1, source_target_pairs={{0,1},{1,0},{2,3},{3,2},{4,5},{5,4},{6,7},{7,6},{8,9},{9,8},{10,11... | collective-permute-start | bytes 196616 | tf_op jit(solution)/shard_map/ppermute | solution.py:47
